TPU v7x, 32 devices: a whole 2x2x4 slice. The times are simulated.
32 devices in a mesh: dev: 32 (over z, y, x, core).
Axes of the slice: x: 2, y: 2, z: 4, core: 2. Of those that a mesh axis runs over, the one named last changes fastest.
Arguments:
- left_table: float32 [65536, 256], P('dev'), may hold values from -6 to 6
- left_state: float32 [65536], P('dev'), may hold values from 0.001 to 0.1
- right_table: float32 [65536, 256], P('dev'), may hold values from -6 to 6
- right_state: float32 [65536], P('dev'), may hold values from 0.001 to 0.1
- relations: float32 [4, 256, 256], replicated, may hold values from -0.375 to 0.375
- relation_state: float32 [4, 256], replicated, may hold values from 819 to 81920
- edge_weights: int32 [32, 4, 16, 128, 128], P('dev'), may hold values from 0 to 3
- tile_left: int32 [32, 4, 16], P('dev'), may hold values from 0 to 15
- tile_right: int32 [32, 4, 16], P('dev'), may hold values from 0 to 15
- tile_relation: int32 [32, 4, 16], P('dev'), may hold values from 0 to 3
- live_count: int32 [32, 4], P('dev'), may hold values from 2 to 16, as said below
Outputs:
- left_out: float32 [65536, 256], P('dev')
- left_state_out: float32 [65536], P('dev')
- right_out: float32 [65536, 256], P('dev')
- right_state_out: float32 [65536], P('dev')
- relations_out: float32 [4, 256, 256], replicated
- relation_state_out: float32 [4, 256], replicated
Inputs may be any that keep to these rules, and one draw needn't show every extreme that they name: `live_count`: in round 0 some partition has exactly 16 live slots.
All inputs are finite; a program needn't handle non-finite values.
Results may differ from a plain program's by a relative error of at most 0.0003.
Values sent between devices are 32-bit elements; how exact they have to be, the bound alone decides.
No kernel may reach another device: no remote copies, remote signals or barrier semaphores. Data moves between devices by JAX's collectives and lax.ppermute only.
A program may use at most 128 MiB of HBM per device.

v0:
```python
import functools

import jax
import jax.numpy as jnp
from jax import lax
from jax.experimental import pallas as pl
from jax.experimental.pallas import tpu as pltpu
from jax.sharding import PartitionSpec as P

learn_rate = 0.1
epsilon = 1e-06
weight_scale = 3.0

F32 = jnp.float32
BF16 = jnp.bfloat16


def split(value):
    high = value.astype(BF16)
    return high, (value - high.astype(F32)).astype(BF16)


def dot3(a, b, dims):
    (ah, al), (bh, bl) = a, b
    d = functools.partial(lax.dot_general, dimension_numbers=(dims, ((), ())), preferred_element_type=F32)
    return d(ah, bh) + (d(ah, bl) + d(al, bh))


NN = ((1,), (0,))
NT = ((1,), (1,))
TN = ((0,), (0,))


def adagrad_tile(table, state_row, grad):
    tile = grad.shape[0]
    eye = lax.broadcasted_iota(jnp.int32, (tile, tile), 0) == lax.broadcasted_iota(jnp.int32, (tile, tile), 1)
    mean = jnp.sum(grad * grad, axis=1, keepdims=True) / grad.shape[1]
    mean_row = jnp.sum(jnp.where(eye, mean, 0.0), axis=0, keepdims=True)
    state_new = state_row + mean_row
    state_col = jnp.sum(jnp.where(eye, state_new, 0.0), axis=1, keepdims=True)
    return table - learn_rate * grad / (jnp.sqrt(state_col) + epsilon), state_new


def bucket_kernel(
    lefts, rights, kinds, count, edges, left, left_state, right, right_state, rel_high, rel_low, rel_in,
    left_out, left_state_out, right_out, right_state_out, rel_out, grad_a, grad_b, used,
):
    tiles, tile = left_state.shape
    width = left.shape[1]
    scale = width ** (-0.5)
    live = count[0]
    rel_out[...] = rel_in[...]
    for t in range(2 * tiles):
        used[t] = 0

    def slot(i, carry):
        ta, tb, kind = lefts[i], rights[i], kinds[i]
        ra = pl.ds(pl.multiple_of(ta * tile, tile), tile)
        rb = pl.ds(pl.multiple_of(tb * tile, tile), tile)

        @pl.when(used[ta] == 0)
        def _():
            grad_a[ra, :] = jnp.zeros((tile, width), F32)

        @pl.when(used[tiles + tb] == 0)
        def _():
            grad_b[rb, :] = jnp.zeros((tile, width), F32)

        used[ta] = 1
        used[tiles + tb] = 1
        a = split(left[ra, :])
        b = split(right[rb, :])
        m = (rel_high[kind], rel_low[kind])
        p = split(dot3(a, m, NN))
        s = dot3(p, b, NT) * scale
        w = edges[i]
        sig = jax.nn.sigmoid(s)
        pos = w.astype(F32) / weight_scale
        g = split((jnp.where(w == 0, sig, 0.0) - pos * jax.nn.sigmoid(-s)) * scale)
        back = split(dot3(g, b, NN))
        grad_b[rb, :] += dot3(g, p, TN)
        grad_a[ra, :] += dot3(back, m, NT)
        rel_out[kind] += dot3(a, back, TN)
        return carry

    lax.fori_loop(0, live, slot, 0)
    left_state_out[...] = left_state[...]
    right_state_out[...] = right_state[...]

    def update(t, carry):
        rows = pl.ds(pl.multiple_of(t * tile, tile), tile)
        for at, table, state, table_out, state_out, grad in (
            (0, left, left_state, left_out, left_state_out, grad_a),
            (tiles, right, right_state, right_out, right_state_out, grad_b),
        ):
            @pl.when(used[at + t] == 0)
            def _():
                table_out[rows, :] = table[rows, :]

            @pl.when(used[at + t] != 0)
            def _():
                new, state_new = adagrad_tile(table[rows, :], state[pl.ds(t, 1), :], grad[rows, :])
                table_out[rows, :] = new
                state_out[pl.ds(t, 1), :] = state_new

        return carry

    lax.fori_loop(0, tiles, update, 0)


def run_bucket(edges, lefts, rights, kinds, count, left, left_state, right, right_state, rel_high, rel_low, rel):
    vmem = pl.BlockSpec(memory_space=pltpu.VMEM)
    smem = pl.BlockSpec(memory_space=pltpu.SMEM)
    like = lambda x: jax.ShapeDtypeStruct(x.shape, x.dtype)
    slots, tile = edges.shape[0], edges.shape[1]
    width = left.shape[1]
    flops = 6 * slots * tile * width * (3 * width + 3 * tile)
    return pl.pallas_call(
        bucket_kernel,
        in_specs=[smem] * 4 + [vmem] * 8,
        out_specs=[vmem] * 5,
        out_shape=[like(left), like(left_state), like(right), like(right_state), like(rel)],
        scratch_shapes=[
            pltpu.VMEM(left.shape, F32),
            pltpu.VMEM(right.shape, F32),
            pltpu.SMEM((2 * left_state.shape[0],), jnp.int32),
        ],
        compiler_params=pltpu.CompilerParams(vmem_limit_bytes=48 * 1024 * 1024),
        cost_estimate=pl.CostEstimate(flops=flops, bytes_accessed=12 * left.size, transcendentals=0),
    )(lefts, rights, kinds, count, edges, left, left_state, right, right_state, rel_high, rel_low, rel)


def shifted(block, axis, distance):
    n = lax.axis_size(axis)
    return lax.ppermute(block, axis, [((i - distance) % n, i) for i in range(n)])


def sum_over(block, axis):
    n = lax.axis_size(axis)
    me = lax.axis_index(axis)
    bits = n.bit_length() - 1
    if n != 1 << bits or block.shape[0] % n:
        return lax.psum(block, axis)
    for b in range(bits):
        mine = ((me >> b) & 1) == 1
        half = block.shape[0] // 2
        low, high = block[:half], block[half:]
        got = lax.ppermute(jnp.where(mine, low, high), axis, [(i, i ^ (1 << b)) for i in range(n)])
        block = jnp.where(mine, high, low) + got
    for b in reversed(range(bits)):
        mine = ((me >> b) & 1) == 1
        got = lax.ppermute(block, axis, [(i, i ^ (1 << b)) for i in range(n)])
        block = jnp.concatenate([jnp.where(mine, got, block), jnp.where(mine, block, got)])
    return block


def adagrad_rows(table, state, grad):
    state_new = state + jnp.mean(grad * grad, axis=1)
    return table - learn_rate * grad / (jnp.sqrt(state_new)[:, None] + epsilon), state_new


def per_device(
    left_table, left_state, right_table, right_state, relations, relation_state,
    edge_weights, tile_left, tile_right, tile_relation, live_count,
):
    edges, lefts, rights, kinds, counts = (
        edge_weights[0], tile_left[0], tile_right[0], tile_relation[0], live_count[0],
    )
    rounds, tile = edges.shape[0], edges.shape[-1]
    rounded = lax.reduce_precision(relations, 8, 7)
    rel_high, rel_low = rounded.astype(BF16), (relations - rounded).astype(BF16)
    rel = jnp.zeros_like(relations)
    left, right = left_table, right_table
    state_l, state_r = left_state.reshape(-1, tile), right_state.reshape(-1, tile)
    for turn in range(rounds):
        left, state_l, right, state_r, rel = run_bucket(
            edges[turn], lefts[turn], rights[turn], kinds[turn], counts[turn : turn + 1],
            left, state_l, right, state_r, rel_high, rel_low, rel,
        )
        if turn + 1 < rounds:
            right, state_r = shifted((right, state_r), "dev", 1)
    right, state_r = shifted((right, state_r), "dev", -(rounds - 1))
    width = relations.shape[-1]
    total = sum_over(rel.reshape(-1, width), "dev")
    new_rel, new_state = adagrad_rows(relations.reshape(-1, width), relation_state.reshape(-1), total)
    return (
        left, state_l.reshape(left_state.shape), right, state_r.reshape(right_state.shape),
        new_rel.reshape(relations.shape), new_state.reshape(relation_state.shape),
    )


def solution(mesh):
    placed = (
        P("dev", None), P("dev"), P("dev", None), P("dev"), P(), P(),
        P("dev", None, None, None, None), P("dev", None, None), P("dev", None, None), P("dev", None, None),
        P("dev", None),
    )
    return jax.shard_map(
        per_device, mesh=mesh, in_specs=placed,
        out_specs=(P("dev", None), P("dev"), P("dev", None), P("dev"), P(), P()), check_vma=False,
    )
```

profile of v0, /device:TPU:1, one launch (start us, length us, event | category | flops | bytes accessed | tf_op | source)
XLA Modules:
  0.0 253.6 jit_solution(13510970722473428479)
XLA Ops:
  0.6 0.8 slice_bitcast_fusion.6
  1.5 1.4 fusion.2
  2.9 2.6 %slice_bitcast_fusion = (s32[16,128,128]{2,1,0:T(8,128)S(1)}, s32[16,128,128]{2,1,0:T(8,128)S(1)}, s32[16,128,128]{2,1,0:T(8,128)S(1)}, s32[16,128,128]{2,1,0:T(8,128)S(1)}) fusion(s32[1,4,16,128,128]{4,3,2,1,0:T(8,128)} %param.17), kind=kLoop, calls=%fused_computation.6 | loop fusion | bytes 8388608 | tf_op jit(solution)/shard_map/squeeze | solution.py:177
  5.5 0.0 copy-done.2
  5.5 0.0 copy-start.5
  5.5 0.0 copy-start.6
  5.5 0.0 copy-start
  5.5 0.0 copy-start.1
  5.5 0.2 fusion
  5.7 0.5 copy-done.5
  6.1 0.0 copy-done.6
  6.2 0.1 broadcast_in_dim.4.rel_in
  6.3 0.0 copy-done
  6.3 8.6 %shard_map.154 = (f32[2048,256]{1,0:T(8,128)}, f32[16,128]{1,0:T(8,128)S(1)}, f32[2048,256]{1,0:T(8,128)}, f32[16,128]{1,0:T(8,128)S(1)}, f32[4,256,256]{2,1,0:T(8,128)S(1)}) custom-call(s32[16]{0:T(128)S(1)} %get-tuple-element.76.lefts, s32[16]{0:T(128)S(1)} %get-tuple-element.87.rights, s32[16]{0:T(128)S(1)} %get-tuple-element.68.kinds, s32[1]{0:T(128)} %bitcast.18.count, ...), custom_call_target="tpu_custom_call" | custom-call | flops 3623878656 | bytes 6291456 | tf_op jit(solution)/shard_map/pallas_call | solution.py:118
  14.9 11.7 %collective-permute-start = (f32[2048,256]{1,0:T(8,128)}, f32[2048,256]{1,0:T(8,128)S(1)}, u32[]{:S(2)}, u32[]{:S(2)}) collective-permute-start(f32[2048,256]{1,0:T(8,128)} %get-tuple-element.28), channel_id=1, source_target_pairs={{31,0},{0,1},{1,2},{2,3},{3,4},{4,5},{5,6},{6,7},{7,8},{8,9},{9,10... | collective-permute-start | bytes 6291464 | tf_op jit(solution)/shard_map/ppermute | solution.py:135
  26.6 0.0 collective-permute-start.1
  26.6 23.3 %collective-permute-done.1.right_state = f32[16,128]{1,0:T(8,128)S(1)} collective-permute-done((f32[16,128]{1,0:T(8,128)S(1)}, f32[16,128]{1,0:T(8,128)S(1)}, u32[]{:S(2)}, u32[]{:S(2)}) %collective-permute-start.1) | collective-permute-done | bytes 8224 | tf_op jit(solution)/shard_map/ppermute | solution.py:135
  49.9 0.0 collective-permute-done.right
  49.9 1.3 copy-done.7
  51.2 8.6 %shard_map.155 = (f32[2048,256]{1,0:T(8,128)}, f32[16,128]{1,0:T(8,128)S(1)}, f32[2048,256]{1,0:T(8,128)}, f32[16,128]{1,0:T(8,128)S(1)}, f32[4,256,256]{2,1,0:T(8,128)S(1)}) custom-call(s32[16]{0:T(128)S(1)} %get-tuple-element.79.lefts, s32[16]{0:T(128)S(1)} %get-tuple-element.84.rights, s32[16]{0:T(128)S(1)} %get-tuple-element.71.kinds, s32[1]{0:T(128)} %bitcast.13.count, ...), custom_call_target="tpu_custom_call" | custom-call | flops 3623878656 | bytes 6291456 | tf_op jit(solution)/shard_map/pallas_call | solution.py:118
  59.8 5.1 %collective-permute-start.2 = (f32[2048,256]{1,0:T(8,128)}, f32[2048,256]{1,0:T(8,128)S(1)}, u32[]{:S(2)}, u32[]{:S(2)}) collective-permute-start(f32[2048,256]{1,0:T(8,128)} %get-tuple-element.33), channel_id=1, source_target_pairs={{31,0},{0,1},{1,2},{2,3},{3,4},{4,5},{5,6},{6,7},{7,8},{8,9},{9,10... | collective-permute-start | bytes 6291464 | tf_op jit(solution)/shard_map/ppermute | solution.py:135
  64.9 0.0 collective-permute-start.3
  64.9 23.3 %collective-permute-done.3.right_state = f32[16,128]{1,0:T(8,128)S(1)} collective-permute-done((f32[16,128]{1,0:T(8,128)S(1)}, f32[16,128]{1,0:T(8,128)S(1)}, u32[]{:S(2)}, u32[]{:S(2)}) %collective-permute-start.3) | collective-permute-done | bytes 8224 | tf_op jit(solution)/shard_map/ppermute | solution.py:135
  88.2 0.0 collective-permute-done.2.right
  88.2 1.3 copy-done.8
  89.5 14.1 %shard_map.156 = (f32[2048,256]{1,0:T(8,128)}, f32[16,128]{1,0:T(8,128)S(1)}, f32[2048,256]{1,0:T(8,128)}, f32[16,128]{1,0:T(8,128)S(1)}, f32[4,256,256]{2,1,0:T(8,128)S(1)}) custom-call(s32[16]{0:T(128)S(1)} %get-tuple-element.77.lefts, s32[16]{0:T(128)S(1)} %get-tuple-element.86.rights, s32[16]{0:T(128)S(1)} %get-tuple-element.69.kinds, s32[1]{0:T(128)} %bitcast.8.count, ...), custom_call_target="tpu_custom_call" | custom-call | flops 3623878656 | bytes 6291456 | tf_op jit(solution)/shard_map/pallas_call | solution.py:118
  103.6 0.0 collective-permute-start.4
  103.6 0.0 collective-permute-start.5
  103.6 23.3 %collective-permute-done.5.right_state = f32[16,128]{1,0:T(8,128)S(1)} collective-permute-done((f32[16,128]{1,0:T(8,128)S(1)}, f32[16,128]{1,0:T(8,128)S(1)}, u32[]{:S(2)}, u32[]{:S(2)}) %collective-permute-start.5) | collective-permute-done | bytes 8224 | tf_op jit(solution)/shard_map/ppermute | solution.py:135
  126.9 0.0 collective-permute-done.4.right
  126.9 12.7 %shard_map.157 = (f32[2048,256]{1,0:T(8,128)}, f32[16,128]{1,0:T(8,128)}, f32[2048,256]{1,0:T(8,128)}, f32[16,128]{1,0:T(8,128)S(1)}, f32[4,256,256]{2,1,0:T(8,128)S(1)}) custom-call(s32[16]{0:T(128)S(1)} %get-tuple-element.78.lefts, s32[16]{0:T(128)S(1)} %get-tuple-element.85.rights, s32[16]{0:T(128)S(1)} %get-tuple-element.70.kinds, s32[1]{0:T(128)} %bitcast.3.count, ...), custom_call_target="tpu_custom_call" | custom-call | flops 3623878656 | bytes 6291456 | tf_op jit(solution)/shard_map/pallas_call | solution.py:118
  139.5 0.1 slice_select_fusion.1
  139.6 1.4 collective-permute-start.8
  141.0 1.5 collective-permute-done.8
  142.5 0.1 bitcast_add_fusion
  142.6 6.6 %collective-permute-start.9 = (f32[256,256]{1,0:T(8,128)S(1)}, f32[256,256]{1,0:T(8,128)S(1)}, u32[]{:S(2)}, u32[]{:S(2)}) collective-permute-start(f32[256,256]{1,0:T(8,128)S(1)} %slice_select_fusion.2), channel_id=1, source_target_pairs={{0,2},{1,3},{2,0},{3,1},{4,6},{5,7},{6,4},{7,5},{8,10},{9,11},{10,... | collective-permute-start | bytes 786440 | tf_op jit(solution)/shard_map/ppermute | solution.py:148
  149.2 6.4 %collective-permute-done.9 = f32[256,256]{1,0:T(8,128)S(1)} collective-permute-done((f32[256,256]{1,0:T(8,128)S(1)}, f32[256,256]{1,0:T(8,128)S(1)}, u32[]{:S(2)}, u32[]{:S(2)}) %collective-permute-start.9) | collective-permute-done | bytes 262176 | tf_op jit(solution)/shard_map/ppermute | solution.py:148
  155.7 9.6 %collective-permute-start.10 = (f32[128,256]{1,0:T(8,128)S(1)}, f32[128,256]{1,0:T(8,128)S(1)}, u32[]{:S(2)}, u32[]{:S(2)}) collective-permute-start(f32[128,256]{1,0:T(8,128)S(1)} %slice_select_fusion.3), channel_id=1, source_target_pairs={{0,4},{1,5},{2,6},{3,7},{4,0},{5,1},{6,2},{7,3},{8,12},{9,13},{10,... | collective-permute-start | bytes 393224 | tf_op jit(solution)/shard_map/ppermute | solution.py:148
  165.3 2.9 %collective-permute-done.10 = f32[128,256]{1,0:T(8,128)S(1)} collective-permute-done((f32[128,256]{1,0:T(8,128)S(1)}, f32[128,256]{1,0:T(8,128)S(1)}, u32[]{:S(2)}, u32[]{:S(2)}) %collective-permute-start.10) | collective-permute-done | bytes 131104 | tf_op jit(solution)/shard_map/ppermute | solution.py:148
  168.2 3.0 %collective-permute-start.11 = (f32[64,256]{1,0:T(8,128)S(1)}, f32[64,256]{1,0:T(8,128)S(1)}, u32[]{:S(2)}, u32[]{:S(2)}) collective-permute-start(f32[64,256]{1,0:T(8,128)S(1)} %slice_select_fusion.4), channel_id=1, source_target_pairs={{0,8},{1,9},{2,10},{3,11},{4,12},{5,13},{6,14},{7,15},{8,0},{9,1},... | collective-permute-start | bytes 196616 | tf_op jit(solution)/shard_map/ppermute | solution.py:148
  171.3 1.7 collective-permute-done.11
  173.0 6.0 %collective-permute-start.12 = (f32[32,256]{1,0:T(8,128)S(1)}, f32[32,256]{1,0:T(8,128)S(1)}, u32[]{:S(2)}, u32[]{:S(2)}) collective-permute-start(f32[32,256]{1,0:T(8,128)S(1)} %slice_select_fusion.5), channel_id=1, source_target_pairs={{0,16},{1,17},{2,18},{3,19},{4,20},{5,21},{6,22},{7,23},{8,24},{9,... | collective-permute-start | bytes 98312 | tf_op jit(solution)/shard_map/ppermute | solution.py:148
  179.0 1.3 collective-permute-done.12
  180.3 2.4 collective-permute-start.13
  182.6 1.3 collective-permute-done.13
  184.0 1.6 collective-permute-start.14
  185.6 1.7 collective-permute-done.14
  187.2 1.0 collective-permute-start.15
  188.3 2.9 %collective-permute-done.15 = f32[128,256]{1,0:T(8,128)S(1)} collective-permute-done((f32[128,256]{1,0:T(8,128)S(1)}, f32[128,256]{1,0:T(8,128)S(1)}, u32[]{:S(2)}, u32[]{:S(2)}) %collective-permute-start.15) | collective-permute-done | bytes 131104 | tf_op jit(solution)/shard_map/ppermute | solution.py:152
  191.2 0.8 collective-permute-start.16
  192.0 11.2 %collective-permute-start.6 = (f32[2048,256]{1,0:T(8,128)}, f32[2048,256]{1,0:T(8,128)}, u32[]{:S(2)}, u32[]{:S(2)}) collective-permute-start(f32[2048,256]{1,0:T(8,128)} %get-tuple-element.43), channel_id=1, source_target_pairs={{3,0},{4,1},{5,2},{6,3},{7,4},{8,5},{9,6},{10,7},{11,8},{12,9},{13... | collective-permute-start | bytes 6291464 | tf_op jit(solution)/shard_map/ppermute | solution.py:135
  203.2 0.0 collective-permute-done.16
  203.3 4.0 %collective-permute-start.17 = (f32[512,256]{1,0:T(8,128)S(1)}, f32[512,256]{1,0:T(8,128)S(1)}, u32[]{:S(2)}, u32[]{:S(2)}) collective-permute-start(f32[512,256]{1,0:T(8,128)S(1)} %pad_maximum_fusion.1), channel_id=1, source_target_pairs={{0,1},{1,0},{2,3},{3,2},{4,5},{5,4},{6,7},{7,6},{8,9},{9,8},{10,11... | collective-permute-start | bytes 1572872 | tf_op jit(solution)/shard_map/ppermute | solution.py:152
  207.4 3.5 %collective-permute-start.7 = (f32[16,128]{1,0:T(8,128)S(1)}, f32[16,128]{1,0:T(8,128)S(1)}, u32[]{:S(2)}, u32[]{:S(2)}) collective-permute-start(f32[16,128]{1,0:T(8,128)S(1)} %get-tuple-element.44), channel_id=1, source_target_pairs={{3,0},{4,1},{5,2},{6,3},{7,4},{8,5},{9,6},{10,7},{11,8},{12,9},{13... | collective-permute-start | bytes 24584 | tf_op jit(solution)/shard_map/ppermute | solution.py:135
  210.9 36.6 %collective-permute-done.7 = f32[16,128]{1,0:T(8,128)S(1)} collective-permute-done((f32[16,128]{1,0:T(8,128)S(1)}, f32[16,128]{1,0:T(8,128)S(1)}, u32[]{:S(2)}, u32[]{:S(2)}) %collective-permute-start.7) | collective-permute-done | bytes 8224 | tf_op jit(solution)/shard_map/ppermute | solution.py:135
  247.5 0.0 collective-permute-done.17
  247.5 0.1 broadcast_select_fusion.1
  247.6 0.2 multiply_reduce_fusion
  247.8 0.4 copy-done.4
  248.2 0.6 sqrt_add_fusion
  248.8 1.2 divide_subtract_fusion
  249.9 0.0 collective-permute-done.6
  250.0 3.0 %copy.19 = f32[2048,256]{1,0:T(8,128)} copy(f32[2048,256]{1,0:T(8,128)} %collective-permute-done.6) | data formatting | bytes 4194304
  253.0 0.6 copy.20
  (26 shorter events, 0.3 us)
Async XLA Ops:
  2.9 2.6 %copy-start.2 = (f32[4,256,256]{2,1,0:T(8,128)S(1)}, f32[4,256,256]{2,1,0:T(8,128)}, u32[]{:S(2)}) copy-start(f32[4,256,256]{2,1,0:T(8,128)} %param.15) | copy-start | bytes 3145732
  5.5 0.7 copy-start.5
  5.5 0.7 copy-start.6
  5.5 0.8 copy-start
  5.5 0.8 copy-start.1
  14.9 35.0 %collective-permute-start = (f32[2048,256]{1,0:T(8,128)}, f32[2048,256]{1,0:T(8,128)S(1)}, u32[]{:S(2)}, u32[]{:S(2)}) collective-permute-start(f32[2048,256]{1,0:T(8,128)} %get-tuple-element.28), channel_id=1, source_target_pairs={{31,0},{0,1},{1,2},{2,3},{3,4},{4,5},{5,6},{6,7},{7,8},{8,9},{9,10... | collective-permute-start | bytes 6291464 | tf_op jit(solution)/shard_map/ppermute | solution.py:135
  26.6 23.3 %collective-permute-start.1 = (f32[16,128]{1,0:T(8,128)S(1)}, f32[16,128]{1,0:T(8,128)S(1)}, u32[]{:S(2)}, u32[]{:S(2)}) collective-permute-start(f32[16,128]{1,0:T(8,128)S(1)} %get-tuple-element.29), channel_id=1, source_target_pairs={{31,0},{0,1},{1,2},{2,3},{3,4},{4,5},{5,6},{6,7},{7,8},{8,9},{9,10... | collective-permute-start | bytes 24584 | tf_op jit(solution)/shard_map/ppermute | solution.py:135
  49.9 1.3 copy-start.7
  59.8 28.4 %collective-permute-start.2 = (f32[2048,256]{1,0:T(8,128)}, f32[2048,256]{1,0:T(8,128)S(1)}, u32[]{:S(2)}, u32[]{:S(2)}) collective-permute-start(f32[2048,256]{1,0:T(8,128)} %get-tuple-element.33), channel_id=1, source_target_pairs={{31,0},{0,1},{1,2},{2,3},{3,4},{4,5},{5,6},{6,7},{7,8},{8,9},{9,10... | collective-permute-start | bytes 6291464 | tf_op jit(solution)/shard_map/ppermute | solution.py:135
  64.9 23.3 %collective-permute-start.3 = (f32[16,128]{1,0:T(8,128)S(1)}, f32[16,128]{1,0:T(8,128)S(1)}, u32[]{:S(2)}, u32[]{:S(2)}) collective-permute-start(f32[16,128]{1,0:T(8,128)S(1)} %get-tuple-element.34), channel_id=1, source_target_pairs={{31,0},{0,1},{1,2},{2,3},{3,4},{4,5},{5,6},{6,7},{7,8},{8,9},{9,10... | collective-permute-start | bytes 24584 | tf_op jit(solution)/shard_map/ppermute | solution.py:135
  88.2 1.3 copy-start.8
  103.6 23.3 %collective-permute-start.4 = (f32[2048,256]{1,0:T(8,128)}, f32[2048,256]{1,0:T(8,128)}, u32[]{:S(2)}, u32[]{:S(2)}) collective-permute-start(f32[2048,256]{1,0:T(8,128)} %get-tuple-element.38), channel_id=1, source_target_pairs={{31,0},{0,1},{1,2},{2,3},{3,4},{4,5},{5,6},{6,7},{7,8},{8,9},{9,10... | collective-permute-start | bytes 6291464 | tf_op jit(solution)/shard_map/ppermute | solution.py:135
  103.6 23.3 %collective-permute-start.5 = (f32[16,128]{1,0:T(8,128)S(1)}, f32[16,128]{1,0:T(8,128)S(1)}, u32[]{:S(2)}, u32[]{:S(2)}) collective-permute-start(f32[16,128]{1,0:T(8,128)S(1)} %get-tuple-element.39), channel_id=1, source_target_pairs={{31,0},{0,1},{1,2},{2,3},{3,4},{4,5},{5,6},{6,7},{7,8},{8,9},{9,10... | collective-permute-start | bytes 24584 | tf_op jit(solution)/shard_map/ppermute | solution.py:135
  139.6 2.9 %collective-permute-start.8 = (f32[512,256]{1,0:T(8,128)S(1)}, f32[512,256]{1,0:T(8,128)S(1)}, u32[]{:S(2)}, u32[]{:S(2)}) collective-permute-start(f32[512,256]{1,0:T(8,128)S(1)} %bitcast.47), channel_id=1, source_target_pairs={{0,1},{1,0},{2,3},{3,2},{4,5},{5,4},{6,7},{7,6},{8,9},{9,8},{10,11... | collective-permute-start | bytes 1572872 | tf_op jit(solution)/shard_map/ppermute | solution.py:148
  142.6 13.0 %collective-permute-start.9 = (f32[256,256]{1,0:T(8,128)S(1)}, f32[256,256]{1,0:T(8,128)S(1)}, u32[]{:S(2)}, u32[]{:S(2)}) collective-permute-start(f32[256,256]{1,0:T(8,128)S(1)} %slice_select_fusion.2), channel_id=1, source_target_pairs={{0,2},{1,3},{2,0},{3,1},{4,6},{5,7},{6,4},{7,5},{8,10},{9,11},{10,... | collective-permute-start | bytes 786440 | tf_op jit(solution)/shard_map/ppermute | solution.py:148
  155.7 12.5 %collective-permute-start.10 = (f32[128,256]{1,0:T(8,128)S(1)}, f32[128,256]{1,0:T(8,128)S(1)}, u32[]{:S(2)}, u32[]{:S(2)}) collective-permute-start(f32[128,256]{1,0:T(8,128)S(1)} %slice_select_fusion.3), channel_id=1, source_target_pairs={{0,4},{1,5},{2,6},{3,7},{4,0},{5,1},{6,2},{7,3},{8,12},{9,13},{10,... | collective-permute-start | bytes 393224 | tf_op jit(solution)/shard_map/ppermute | solution.py:148
  168.2 4.7 %collective-permute-start.11 = (f32[64,256]{1,0:T(8,128)S(1)}, f32[64,256]{1,0:T(8,128)S(1)}, u32[]{:S(2)}, u32[]{:S(2)}) collective-permute-start(f32[64,256]{1,0:T(8,128)S(1)} %slice_select_fusion.4), channel_id=1, source_target_pairs={{0,8},{1,9},{2,10},{3,11},{4,12},{5,13},{6,14},{7,15},{8,0},{9,1},... | collective-permute-start | bytes 196616 | tf_op jit(solution)/shard_map/ppermute | solution.py:148
  173.0 7.3 %collective-permute-start.12 = (f32[32,256]{1,0:T(8,128)S(1)}, f32[32,256]{1,0:T(8,128)S(1)}, u32[]{:S(2)}, u32[]{:S(2)}) collective-permute-start(f32[32,256]{1,0:T(8,128)S(1)} %slice_select_fusion.5), channel_id=1, source_target_pairs={{0,16},{1,17},{2,18},{3,19},{4,20},{5,21},{6,22},{7,23},{8,24},{9,... | collective-permute-start | bytes 98312 | tf_op jit(solution)/shard_map/ppermute | solution.py:148
  180.3 3.7 %collective-permute-start.13 = (f32[32,256]{1,0:T(8,128)S(1)}, f32[32,256]{1,0:T(8,128)S(1)}, u32[]{:S(2)}, u32[]{:S(2)}) collective-permute-start(f32[32,256]{1,0:T(8,128)S(1)} %select_add_fusion.3), channel_id=1, source_target_pairs={{0,16},{1,17},{2,18},{3,19},{4,20},{5,21},{6,22},{7,23},{8,24},{9,... | collective-permute-start | bytes 98312 | tf_op jit(solution)/shard_map/ppermute | solution.py:152
  184.0 3.2 %collective-permute-start.14 = (f32[64,256]{1,0:T(8,128)S(1)}, f32[64,256]{1,0:T(8,128)S(1)}, u32[]{:S(2)}, u32[]{:S(2)}) collective-permute-start(f32[64,256]{1,0:T(8,128)S(1)} %pad_maximum_fusion.4), channel_id=1, source_target_pairs={{0,8},{1,9},{2,10},{3,11},{4,12},{5,13},{6,14},{7,15},{8,0},{9,1},... | collective-permute-start | bytes 196616 | tf_op jit(solution)/shard_map/ppermute | solution.py:152
  187.2 3.9 %collective-permute-start.15 = (f32[128,256]{1,0:T(8,128)S(1)}, f32[128,256]{1,0:T(8,128)S(1)}, u32[]{:S(2)}, u32[]{:S(2)}) collective-permute-start(f32[128,256]{1,0:T(8,128)S(1)} %pad_maximum_fusion.3), channel_id=1, source_target_pairs={{0,4},{1,5},{2,6},{3,7},{4,0},{5,1},{6,2},{7,3},{8,12},{9,13},{10,... | collective-permute-start | bytes 393224 | tf_op jit(solution)/shard_map/ppermute | solution.py:152
  191.2 12.1 %collective-permute-start.16 = (f32[256,256]{1,0:T(8,128)S(1)}, f32[256,256]{1,0:T(8,128)S(1)}, u32[]{:S(2)}, u32[]{:S(2)}) collective-permute-start(f32[256,256]{1,0:T(8,128)S(1)} %pad_maximum_fusion.2), channel_id=1, source_target_pairs={{0,2},{1,3},{2,0},{3,1},{4,6},{5,7},{6,4},{7,5},{8,10},{9,11},{10,... | collective-permute-start | bytes 786440 | tf_op jit(solution)/shard_map/ppermute | solution.py:152
  192.0 57.9 %collective-permute-start.6 = (f32[2048,256]{1,0:T(8,128)}, f32[2048,256]{1,0:T(8,128)}, u32[]{:S(2)}, u32[]{:S(2)}) collective-permute-start(f32[2048,256]{1,0:T(8,128)} %get-tuple-element.43), channel_id=1, source_target_pairs={{3,0},{4,1},{5,2},{6,3},{7,4},{8,5},{9,6},{10,7},{11,8},{12,9},{13... | collective-permute-start | bytes 6291464 | tf_op jit(solution)/shard_map/ppermute | solution.py:135
  203.3 44.2 %collective-permute-start.17 = (f32[512,256]{1,0:T(8,128)S(1)}, f32[512,256]{1,0:T(8,128)S(1)}, u32[]{:S(2)}, u32[]{:S(2)}) collective-permute-start(f32[512,256]{1,0:T(8,128)S(1)} %pad_maximum_fusion.1), channel_id=1, source_target_pairs={{0,1},{1,0},{2,3},{3,2},{4,5},{5,4},{6,7},{7,6},{8,9},{9,8},{10,11... | collective-permute-start | bytes 1572872 | tf_op jit(solution)/shard_map/ppermute | solution.py:152
  207.4 40.1 %collective-permute-start.7 = (f32[16,128]{1,0:T(8,128)S(1)}, f32[16,128]{1,0:T(8,128)S(1)}, u32[]{:S(2)}, u32[]{:S(2)}) collective-permute-start(f32[16,128]{1,0:T(8,128)S(1)} %get-tuple-element.44), channel_id=1, source_target_pairs={{3,0},{4,1},{5,2},{6,3},{7,4},{8,5},{9,6},{10,7},{11,8},{12,9},{13... | collective-permute-start | bytes 24584 | tf_op jit(solution)/shard_map/ppermute | solution.py:135
  247.5 0.7 copy-start.4
  247.5 1.3 copy-start.3
where the time goes:
time: 258 us; the launch traced here: 254 us
  waiting for transfers between devices  126 us (49%)
  starting transfers between devices  68 us (26%)
  Pallas kernels  43.9 us (17%)
  local copies, waits for them, and re-layouts  12.1 us (5%)
  other arithmetic  2.69 us (1%)
    ppermute x8, waiting for transfers between devices, shifted(): lax.ppermute(block, axis, [((i - distance) % n, i) for i in range(n)])  106 us
    pallas_call x4, Pallas kernels, run_bucket(): pl.pallas_call(bucket_kernel, in_specs=[smem] * 4 + [vmem] * 8, out_specs...  43.9 us
    ppermute x8, starting transfers between devices, shifted(): lax.ppermute(block, axis, [((i - distance) % n, i) for i in range(n)])  31.6 us
    ppermute x5, starting transfers between devices, sum_over(): lax.ppermute(jnp.where(mine, low, high), axis, [(i, i ^ 1 << b) for i in...  26.6 us
    ppermute x5, waiting for transfers between devices, sum_over(): lax.ppermute(jnp.where(mine, low, high), axis, [(i, i ^ 1 << b) for i in...  13.8 us
    ppermute x5, starting transfers between devices, sum_over(): got = lax.ppermute(block, axis, [(i, i ^ 1 << b) for i in range(n)])  9.84 us
    unnamed x20, local copies, waits for them, and re-layouts  7.16 us
    ppermute x5, waiting for transfers between devices, sum_over(): got = lax.ppermute(block, axis, [(i, i ^ 1 << b) for i in range(n)])  5.82 us
  transfers between devices with their start and end apart: 18, of which 12 were waited for; matrix products, arithmetic and copies ran while one was open for 1% of the time, Pallas kernels for 0%

commit v1 on v0

v1 whole, which is shorter than its diff:
```python
import functools

import jax
import jax.numpy as jnp
from jax import lax
from jax.experimental import pallas as pl
from jax.experimental.pallas import tpu as pltpu
from jax.sharding import PartitionSpec as P

learn_rate = 0.1
epsilon = 1e-06
weight_scale = 3.0

F32 = jnp.float32
BF16 = jnp.bfloat16
PARTS = 2
TOGETHER = 2
UPDATES = 4

NN = ((1,), (0,))
NT = ((1,), (1,))
TN = ((0,), (0,))


def split(value):
    high = value.astype(BF16)
    return high, (value - high.astype(F32)).astype(BF16)


def dot3(a, b, dims):
    (ah, al), (bh, bl) = a, b
    ca, cb = dims[0][0], dims[1][0]
    return lax.dot_general(
        jnp.concatenate([ah, ah, al], axis=ca),
        jnp.concatenate([bh, bl, bh], axis=cb),
        (dims, ((), ())),
        preferred_element_type=F32,
    )


def dscore(s, w, scale):
    small = jnp.exp(-jnp.abs(s))
    large_part = 1.0 / (1.0 + small)
    small_part = small * large_part
    up = s >= 0
    sig = jnp.where(up, large_part, small_part)
    anti = jnp.where(up, small_part, large_part)
    return jnp.where(w == 0, sig, anti * (w.astype(F32) * (-1.0 / weight_scale))) * scale


def adagrad_tile(table, state_row, grad):
    tile, width = grad.shape
    eye = lax.broadcasted_iota(jnp.int32, (tile, tile), 0) == lax.broadcasted_iota(jnp.int32, (tile, tile), 1)
    mean = jnp.sum(grad * grad, axis=1, keepdims=True) / width
    state_new = state_row + jnp.sum(jnp.where(eye, mean, 0.0), axis=0, keepdims=True)
    rate_row = learn_rate / (jnp.sqrt(state_new) + epsilon)
    rate = jnp.sum(jnp.where(eye, rate_row, 0.0), axis=1, keepdims=True)
    return table - grad * rate, state_new


def bucket_kernel(turn, part, first, dims, lefts, rights, kinds, count, edges, *refs):
    tiles, per_part, tile, width, kinds_count = dims
    last = part == PARTS - 1
    refs = list(refs)
    left = refs.pop(0)
    state_l = refs.pop(0) if last else None
    right = refs.pop(0)
    state_r = refs.pop(0) if first else None
    operators = refs.pop(0)
    rel = None if first and part == 0 else refs.pop(0)
    handed = refs.pop(0) if last else None
    if last:
        left_out, state_l_out = refs.pop(0), refs.pop(0)
    right_out, rel_out = refs.pop(0), refs.pop(0)
    handed_out = None if last else refs.pop(0)
    (weights, held, grads, states, maps, highs, lows, grad_r, seen, order, todo, sem_w, sem_t, sem_g, sem_k, sem_s) = refs
    fill = first and last
    scale = width ** (-0.5)
    live = count[0, turn]
    spare = tiles + per_part
    kind_at = spare

    def rows(t):
        return pl.ds(pl.multiple_of(t * tile, tile), tile)

    def load_left(t):
        return pltpu.make_async_copy(left.at[rows(t)], held.at[rows(t)], sem_t.at[t])

    def store_left(t):
        return pltpu.make_async_copy(held.at[rows(t)], left_out.at[rows(t)], sem_t.at[t])

    def load_right(t):
        at = tiles + t
        source = right.at[rows(part * per_part + t)] if first else right.at[rows(t)]
        return pltpu.make_async_copy(source, held.at[rows(at)], sem_t.at[at])

    def store_right(t):
        at = tiles + t
        return pltpu.make_async_copy(held.at[rows(at)], right_out.at[rows(t)], sem_t.at[at])

    def take(t):
        return pltpu.make_async_copy(handed.at[rows(t)], grads.at[rows(t)], sem_g.at[t])

    def hand(t):
        return pltpu.make_async_copy(grads.at[rows(t)], handed_out.at[rows(t)], sem_g.at[t])

    def load_weights(i):
        return pltpu.make_async_copy(edges.at[0, turn, i], weights.at[i], sem_w.at[i])

    def load_kind(kind):
        copies = [pltpu.make_async_copy(operators.at[kind], maps.at[kind], sem_k.at[0, kind])]
        if rel is not None:
            copies.append(pltpu.make_async_copy(rel.at[kind], grad_r.at[kind], sem_k.at[1, kind]))
        return copies

    def store_kind(kind):
        return pltpu.make_async_copy(grad_r.at[kind], rel_out.at[kind], sem_k.at[1, kind])

    held_r = states.at[pl.ds(tiles, per_part)]
    packed = pl.ds(per_part * tile, per_part), pl.ds(0, tile)
    source = state_r.at[pl.ds(part * per_part, per_part)] if first else right.at[packed]
    load_states = [pltpu.make_async_copy(source, held_r, sem_s.at[0])]
    store_states = [pltpu.make_async_copy(held_r, right_out.at[packed], sem_s.at[0])]
    if last:
        held_l = states.at[pl.ds(0, tiles)]
        load_states.append(pltpu.make_async_copy(state_l, held_l, sem_s.at[1]))
        store_states.append(pltpu.make_async_copy(held_l, state_l_out, sem_s.at[1]))

    for t in range(spare + kinds_count):
        seen[t] = 0
    for t in range(spare + UPDATES):
        order[t] = spare
    used = jnp.int32(0)

    def mine(i):
        return rights[0, turn, i] // per_part == part

    def ask(i, carry):
        used, jobs = carry
        now = mine(i)
        a, b, kind = lefts[0, turn, i], rights[0, turn, i] - part * per_part, kinds[0, turn, i]
        new_a = now & (seen[a] == 0)
        new_b = now & (seen[jnp.where(now, tiles + b, 0)] == 0)

        @pl.when(now)
        def _():
            todo[jobs] = i
            load_weights(i).start()

            @pl.when(seen[kind_at + kind] == 0)
            def _():
                for copy in load_kind(kind):
                    copy.start()
                seen[kind_at + kind] = 1

        @pl.when(new_a)
        def _():
            load_left(a).start()
            seen[a] = 1
            grads[rows(a), :] = jnp.zeros((tile, width), F32)
            if last:
                order[used] = a

        if last:
            used = used + new_a.astype(jnp.int32)

        @pl.when(new_b)
        def _():
            load_right(b).start()
            seen[tiles + b] = 1
            grads[rows(tiles + b), :] = jnp.zeros((tile, width), F32)
            order[used] = tiles + b

        return used + new_b.astype(jnp.int32), jobs + now.astype(jnp.int32)

    if last:
        def ask_handed(i, used):
            a = lefts[0, turn, i]
            new = jnp.logical_not(mine(i)) & (seen[a] == 0)

            @pl.when(new)
            def _():
                load_left(a).start()
                take(a).start()
                seen[a] = 4
                order[used] = a

            return used + new.astype(jnp.int32)

        used = lax.fori_loop(0, live, ask_handed, used)
    used, jobs = lax.fori_loop(0, live, ask, (used, jnp.int32(0)))
    states[pl.ds(spare, 8), :] = jnp.ones((8, tile), F32)
    for copy in load_states:
        copy.start()
    if rel is None:
        grad_r[...] = jnp.zeros_like(grad_r)

    def each_unseen(side_count, base, act):
        def body(t, carry):
            pl.when(seen[base + t] == 0)(lambda: act(t))
            return carry

        lax.fori_loop(0, side_count, body, 0)

    if fill:
        each_unseen(tiles, 0, lambda t: load_left(t).start())
    if first:
        each_unseen(per_part, tiles, lambda t: load_right(t).start())
    held[rows(spare), :] = jnp.zeros((tile, width), F32)
    grads[rows(spare), :] = jnp.zeros((tile, width), F32)

    def arrive_left(a):
        @pl.when(seen[a] == 1)
        def _():
            load_left(a).wait()
            seen[a] = 2

        if last:
            @pl.when(seen[a] == 4)
            def _():
                load_left(a).wait()
                take(a).wait()
                seen[a] = 2

    def arrive(i):
        arrive_left(lefts[0, turn, i])
        b, kind = rights[0, turn, i] - part * per_part, kinds[0, turn, i]

        @pl.when(seen[tiles + b] == 1)
        def _():
            load_right(b).wait()
            seen[tiles + b] = 2

        @pl.when(seen[kind_at + kind] == 1)
        def _():
            for copy in load_kind(kind):
                copy.wait()
            highs[kind], lows[kind] = split(maps[kind])
            seen[kind_at + kind] = 2

        load_weights(i).wait()

    def group(j, carry):
        places = [j * TOGETHER + n for n in range(TOGETHER)]
        slots = [todo[jnp.minimum(place, jobs - 1)] for place in places]
        arrive(slots[0])
        for i, place in zip(slots[1:], places[1:]):
            pl.when(place < jobs)(functools.partial(arrive, i))
        work = [
            (
                jnp.where(place < jobs, lefts[0, turn, i], spare),
                jnp.where(place < jobs, tiles + rights[0, turn, i] - part * per_part, spare),
                kinds[0, turn, i],
            )
            for i, place in zip(slots, places)
        ]
        a = [split(held[rows(ta), :]) for ta, _, _ in work]
        b = [split(held[rows(tb), :]) for _, tb, _ in work]
        m = [(highs[kind], lows[kind]) for _, _, kind in work]
        p = [split(dot3(x, y, NN)) for x, y in zip(a, m)]
        s = [dot3(x, y, NT) * scale for x, y in zip(p, b)]
        g = [split(dscore(x, weights[i], scale)) for x, i in zip(s, slots)]
        back = [split(dot3(x, y, NN)) for x, y in zip(g, b)]
        term_b = [dot3(x, y, TN) for x, y in zip(g, p)]
        term_a = [dot3(x, y, NT) for x, y in zip(back, m)]
        term_r = [dot3(x, y, TN) for x, y in zip(a, back)]
        for (ta, tb, kind), x, y, z in zip(work, term_a, term_b, term_r):
            grads[rows(ta), :] += x
            grads[rows(tb), :] += y
            grad_r[kind] += z
        return carry

    lax.fori_loop(0, (jobs + TOGETHER - 1) // TOGETHER, group, 0)

    def each_kind(act):
        for kind in range(kinds_count):
            if rel is None:
                act(store_kind(kind))
            else:
                pl.when(seen[kind_at + kind] == 2)(functools.partial(act, store_kind(kind)))

    each_kind(lambda copy: copy.start())
    if first:
        each_unseen(per_part, tiles, lambda t: (load_right(t).wait(), store_right(t).start()) and None)
    if last:
        def settle_handed(t, carry):
            arrive_left(t)
            return carry

        lax.fori_loop(0, tiles, settle_handed, 0)
        if fill:
            each_unseen(tiles, 0, lambda t: (load_left(t).wait(), store_left(t).start()) and None)

    for copy in load_states:
        copy.wait()

    def update(j, carry):
        places = [order[j * UPDATES + n] for n in range(UPDATES)]
        done = [adagrad_tile(held[rows(at), :], states[pl.ds(at, 1), :], grads[rows(at), :]) for at in places]
        for at, (new, state_new) in zip(places, done):
            held[rows(at), :] = new
            states[pl.ds(at, 1), :] = state_new
            if last:
                pl.when(at < tiles)(lambda: store_left(at).start())
            pl.when((at >= tiles) & (at < spare))(lambda: store_right(at - tiles).start())
        return carry

    def each_touched(side_count, base, act):
        def body(t, carry):
            pl.when(seen[base + t] == 2)(lambda: act(t))
            return carry

        lax.fori_loop(0, side_count, body, 0)

    if not last:
        each_touched(tiles, 0, lambda t: hand(t).start())
    lax.fori_loop(0, (used + UPDATES - 1) // UPDATES, update, 0)
    for copy in store_states:
        copy.start()
    if not last:
        each_touched(tiles, 0, lambda t: hand(t).wait())
    else:
        each_touched(tiles, 0, lambda t: store_left(t).wait())
    each_touched(per_part, tiles, lambda t: store_right(t).wait())
    if fill:
        each_unseen(tiles, 0, lambda t: store_left(t).wait())
    if first:
        each_unseen(per_part, tiles, lambda t: store_right(t).wait())
    for copy in store_states:
        copy.wait()
    each_kind(lambda copy: copy.wait())


def run_part(turn, part, edges, lefts, rights, kinds, count, left, state_l, right, state_r, operators, rel, handed):
    first, last = state_r is not None, part == PARTS - 1
    anywhere = pl.BlockSpec(memory_space=pl.ANY)
    smem = pl.BlockSpec(memory_space=pltpu.SMEM)
    slots, tile = edges.shape[2], edges.shape[3]
    tiles, width = state_l.shape[0], left.shape[1]
    per_part = tiles // PARTS
    kinds_count = operators.shape[0]
    rows = (tiles + per_part + 1) * tile
    dma = pltpu.SemaphoreType.DMA
    shape = lambda *dims: jax.ShapeDtypeStruct(dims, F32)
    names = [("lefts", lefts), ("rights", rights), ("kinds", kinds), ("count", count), ("edges", edges), ("left", left)]
    names += [("state_l", state_l)] if last else []
    names += [("right", right)]
    names += [("state_r", state_r)] if first else []
    names += [("operators", operators)]
    names += [("rel", rel)] if rel is not None else []
    names += [("handed", handed)] if last else []
    outs = [("left", shape(*left.shape)), ("state_l", shape(*state_l.shape))] if last else []
    outs += [("right", shape(per_part * (tile + 1), width)), ("rel", shape(*operators.shape))]
    outs += [] if last else [("handed", shape(*left.shape))]
    place = {name: i for i, (name, _) in enumerate(names)}
    shared = {
        place[name]: i for i, (name, _) in enumerate(outs)
        if name in place and (name == "rel" or not first)
    }
    new = pl.pallas_call(
        functools.partial(bucket_kernel, turn, part, first, (tiles, per_part, tile, width, kinds_count)),
        in_specs=[smem] * 4 + [anywhere] * (len(names) - 4),
        out_specs=[anywhere] * len(outs),
        out_shape=[out for _, out in outs],
        input_output_aliases=shared,
        scratch_shapes=[
            pltpu.VMEM((slots, tile, tile), jnp.int32),
            pltpu.VMEM((rows, width), F32),
            pltpu.VMEM((rows, width), F32),
            pltpu.VMEM((tiles + per_part + 8, tile), F32),
            pltpu.VMEM(operators.shape, F32),
            pltpu.VMEM(operators.shape, BF16),
            pltpu.VMEM(operators.shape, BF16),
            pltpu.VMEM(operators.shape, F32),
            pltpu.SMEM((tiles + per_part + kinds_count,), jnp.int32),
            pltpu.SMEM((tiles + per_part + UPDATES,), jnp.int32),
            pltpu.SMEM((slots,), jnp.int32),
            dma((slots,)),
            dma((tiles + per_part,)),
            dma((tiles,)),
            dma((2, kinds_count)),
            dma((2,)),
        ],
        compiler_params=pltpu.CompilerParams(vmem_limit_bytes=60 * 1024 * 1024),
        cost_estimate=pl.CostEstimate(flops=4 * 10**9, bytes_accessed=4 * left.size, transcendentals=0),
    )(*[value for _, value in names])
    return dict(zip([name for name, _ in outs], new))


def unpack_kernel(*refs):
    parts, (table, state), (sems,) = refs[:PARTS], refs[PARTS : PARTS + 2], refs[PARTS + 2 :]
    body = table.shape[0] // PARTS
    per_part, tile = state.shape[0] // PARTS, state.shape[1]
    copies = []
    for n, part in enumerate(parts):
        copies.append(
            pltpu.make_async_copy(part.at[pl.ds(0, body)], table.at[pl.ds(n * body, body)], sems.at[2 * n])
        )
        copies.append(
            pltpu.make_async_copy(
                part.at[pl.ds(body, per_part), pl.ds(0, tile)], state.at[pl.ds(n * per_part, per_part)],
                sems.at[2 * n + 1],
            )
        )
    for copy in copies:
        copy.start()
    for copy in copies:
        copy.wait()


def unpack(parts, table, state):
    return pl.pallas_call(
        unpack_kernel,
        in_specs=[pl.BlockSpec(memory_space=pltpu.VMEM)] * PARTS,
        out_specs=[pl.BlockSpec(memory_space=pl.ANY)] * 2,
        out_shape=[jax.ShapeDtypeStruct(table, F32), jax.ShapeDtypeStruct(state, F32)],
        scratch_shapes=[pltpu.SemaphoreType.DMA((2 * PARTS,))],
        compiler_params=pltpu.CompilerParams(vmem_limit_bytes=16 * 1024 * 1024),
    )(*parts)


def shifted(block, axis, distance):
    n = lax.axis_size(axis)
    return lax.ppermute(block, axis, [(i, (i + distance) % n) for i in range(n)])


def sum_over(block, axis, sends, distance):
    n = lax.axis_size(axis)
    bits = n.bit_length() - 1
    if n != 1 << bits or block.shape[0] % n:
        return lax.psum(block, axis), [shifted(x, axis, distance) for x in sends]
    me = lax.axis_index(axis)
    digits, at = [], 0
    while at < bits:
        wide = 1 if at == 0 else min(2, bits - at)
        digits.append((at, 1 << wide))
        at += wide
    sends, arrived = list(sends), {0: shifted(sends[0], axis, distance)}
    plan = iter([((), ()), ((), (0,)), ((1,), ()), ((), ()), ((), (1,))])

    def tie(block):
        send, want = next(plan, ((), ()))
        for which in send:
            block, sends[which] = lax.optimization_barrier((block, sends[which]))
            arrived[which] = shifted(sends[which], axis, distance)
        for which in want:
            block, arrived[which] = lax.optimization_barrier((block, arrived[which]))
        return block

    for at, size in digits:
        block = tie(block)
        mine = (me >> at) & (size - 1)
        parts = block.reshape(size, -1, block.shape[1])
        got = [
            lax.ppermute(
                lax.dynamic_index_in_dim(parts, mine ^ j, keepdims=False), axis,
                [(i, i ^ (j << at)) for i in range(n)],
            )
            for j in range(1, size)
        ]
        block = lax.dynamic_index_in_dim(parts, mine, keepdims=False)
        for other in got:
            block = block + other
    for at, size in reversed(digits):
        block = tie(block)
        mine = (me >> at) & (size - 1)
        got = [block] + [lax.ppermute(block, axis, [(i, i ^ (j << at)) for i in range(n)]) for j in range(1, size)]
        whole = jnp.zeros((size,) + block.shape, block.dtype)
        for j, other in enumerate(got):
            whole = lax.dynamic_update_index_in_dim(whole, other, mine ^ j, 0)
        block = whole.reshape(-1, block.shape[1])
    tie(block)
    return block, [arrived.get(i) if i in arrived else shifted(x, axis, distance) for i, x in enumerate(sends)]


def adagrad_rows(table, state, grad):
    state_new = state + jnp.mean(grad * grad, axis=1)
    return table - learn_rate * grad / (jnp.sqrt(state_new)[:, None] + epsilon), state_new


def per_device(
    left_table, left_state, right_table, right_state, relations, relation_state,
    edge_weights, tile_left, tile_right, tile_relation, live_count,
):
    rounds, tile = edge_weights.shape[1], edge_weights.shape[-1]
    left, state_l = left_table, left_state.reshape(-1, tile)
    rights_now = [right_table] * PARTS
    state_r = right_state.reshape(-1, tile)
    rel = None
    for turn in range(rounds):
        handed = None
        for part in range(PARTS):
            new = run_part(
                turn, part, edge_weights, tile_left, tile_right, tile_relation, live_count,
                left, state_l, rights_now[part], state_r if turn == 0 else None, relations, rel, handed,
            )
            rel, handed = new["rel"], new.get("handed")
            rights_now[part] = shifted(new["right"], "dev", 1) if turn + 1 < rounds else new["right"]
        left, state_l = new["left"], new["state_l"]
    width = relations.shape[-1]
    total, rights_now = sum_over(rel.reshape(-1, width), "dev", rights_now, 1 - rounds)
    right, state_r = unpack(rights_now, right_table.shape, (right_state.shape[0] // tile, tile))
    new_rel, new_state = adagrad_rows(relations.reshape(-1, width), relation_state.reshape(-1), total)
    return (
        left, state_l.reshape(left_state.shape), right, state_r.reshape(right_state.shape),
        new_rel.reshape(relations.shape), new_state.reshape(relation_state.shape),
    )


def solution(mesh):
    placed = (
        P("dev", None), P("dev"), P("dev", None), P("dev"), P(), P(),
        P("dev", None, None, None, None), P("dev", None, None), P("dev", None, None), P("dev", None, None),
        P("dev", None),
    )
    return jax.shard_map(
        per_device, mesh=mesh, in_specs=placed,
        out_specs=(P("dev", None), P("dev"), P("dev", None), P("dev"), P(), P()), check_vma=False,
    )
```

time: 258 us -> 169 us (0.66)
  the two profiles are of different devices: /device:TPU:1 before, /device:TPU:17 now
where the time goes in v1:
time: 169 us; the launch traced here: 166 us
  starting transfers between devices  58.6 us (35%)
  waiting for transfers between devices  51.8 us (31%)
  Pallas kernels  44.6 us (26%)
  local copies, waits for them, and re-layouts  7.84 us (5%)
  other arithmetic  2.14 us (1%)
    pallas_call x8, Pallas kernels, run_part(): pl.pallas_call(functools.partial(bucket_kernel, turn, part, first, (tiles...  43.3 us
    ppermute x7, waiting for transfers between devices, sum_over(): lax.ppermute(lax.dynamic_index_in_dim(parts, mine ^ j, keepdims=False), a...  31.3 us
    ppermute x7, starting transfers between devices, sum_over(): lax.ppermute(lax.dynamic_index_in_dim(parts, mine ^ j, keepdims=False), a...  27.7 us
    ppermute x8, starting transfers between devices, shifted(): lax.ppermute(block, axis, [(i, (i + distance) % n) for i in range(n)])  22.3 us
    ppermute x8, waiting for transfers between devices, shifted(): lax.ppermute(block, axis, [(i, (i + distance) % n) for i in range(n)])  14.7 us
    ppermute x7, starting transfers between devices, sum_over(): lax.ppermute(block, axis, [(i, i ^ j << at) for i in range(n)])  8.55 us
    unnamed x20, local copies, waits for them, and re-layouts  6.36 us
    ppermute x7, waiting for transfers between devices, sum_over(): lax.ppermute(block, axis, [(i, i ^ j << at) for i in range(n)])  5.88 us
  transfers between devices with their start and end apart: 22, of which 17 were waited for; matrix products, arithmetic and copies ran while one was open for 1% of the time, Pallas kernels for 24%

profile of v1, /device:TPU:17, one launch (start us, length us, event | category | flops | bytes accessed | tf_op | source)
XLA Modules:
  0.0 165.9 jit_solution(10163755017944643962)
XLA Ops:
  0.6 5.1 %shard_map.154 = (f32[1032,256]{1,0:T(8,128)}, f32[4,256,256]{2,1,0:T(8,128)}, f32[2048,256]{1,0:T(8,128)}) custom-call(s32[1,4,16]{2,1,0:T(4,128)} %lefts.15, s32[1,4,16]{2,1,0:T(4,128)} %rights.15, s32[1,4,16]{2,1,0:T(4,128)} %kinds.15, s32[1,4]{1,0:T(1,128)} %count.15, s32[1,4,16,128,128]{4,3,2,1,0:T(8,128)} %edges.15, f32[2048,256]{1,0:T(8,128)} %refs_0_.3, ...), custom_call_target="tpu_custom_call" | custom-call | flops 4000000000 | bytes 2097152 | tf_op jit(solution)/shard_map/pallas_call | solution.py:360
  5.7 1.8 %collective-permute-start.1 = (f32[1032,256]{1,0:T(8,128)}, f32[1032,256]{1,0:T(8,128)S(1)}, u32[]{:S(2)}, u32[]{:S(2)}) collective-permute-start(f32[1032,256]{1,0:T(8,128)} %get-tuple-element.47), channel_id=1, source_target_pairs={{0,1},{1,2},{2,3},{3,4},{4,5},{5,6},{6,7},{7,8},{8,9},{9,10},{10,1... | collective-permute-start | bytes 3170312 | tf_op jit(solution)/shard_map/ppermute | solution.py:424
  7.6 6.2 %shard_map.155 = (f32[2048,256]{1,0:T(8,128)}, f32[16,128]{1,0:T(8,128)}, f32[1032,256]{1,0:T(8,128)}, f32[4,256,256]{2,1,0:T(8,128)}) custom-call(s32[1,4,16]{2,1,0:T(4,128)} %lefts.15, s32[1,4,16]{2,1,0:T(4,128)} %rights.15, s32[1,4,16]{2,1,0:T(4,128)} %kinds.15, s32[1,4]{1,0:T(1,128)} %count.15, ...), custom_call_target="tpu_custom_call", output_to_operand_aliasing={{3}: (10, {})} | custom-call | flops 4000000000 | bytes 2097152 | tf_op jit(solution)/shard_map/pallas_call | solution.py:360
  13.7 1.1 collective-permute-start
  14.9 4.8 %collective-permute-done.1.refs_1_ = f32[1032,256]{1,0:T(8,128)S(1)} collective-permute-done((f32[1032,256]{1,0:T(8,128)}, f32[1032,256]{1,0:T(8,128)S(1)}, u32[]{:S(2)}, u32[]{:S(2)}) %collective-permute-start.1) | collective-permute-done | bytes 1056800 | tf_op jit(solution)/shard_map/ppermute | solution.py:424
  19.7 1.0 copy-done.9
  20.7 6.5 %shard_map.156 = (f32[1032,256]{1,0:T(8,128)}, f32[4,256,256]{2,1,0:T(8,128)}, f32[2048,256]{1,0:T(8,128)}) custom-call(s32[1,4,16]{2,1,0:T(4,128)} %lefts.15, s32[1,4,16]{2,1,0:T(4,128)} %rights.15, s32[1,4,16]{2,1,0:T(4,128)} %kinds.15, s32[1,4]{1,0:T(1,128)} %count.15, ...), custom_call_target="tpu_custom_call", output_to_operand_aliasing={{0}: (6, {}), {1}: (8, {})} | custom-call | flops 4000000000 | bytes 2097152 | tf_op jit(solution)/shard_map/pallas_call | solution.py:360
  27.2 0.8 collective-permute-start.3
  28.0 3.0 %collective-permute-done.refs_2_ = f32[1032,256]{1,0:T(8,128)S(1)} collective-permute-done((f32[1032,256]{1,0:T(8,128)}, f32[1032,256]{1,0:T(8,128)S(1)}, u32[]{:S(2)}, u32[]{:S(2)}) %collective-permute-start) | collective-permute-done | bytes 1056800 | tf_op jit(solution)/shard_map/ppermute | solution.py:424
  31.0 1.0 copy-done.7
  32.0 3.7 %shard_map.157 = (f32[2048,256]{1,0:T(8,128)}, f32[16,128]{1,0:T(8,128)}, f32[1032,256]{1,0:T(8,128)}, f32[4,256,256]{2,1,0:T(8,128)}) custom-call(s32[1,4,16]{2,1,0:T(4,128)} %lefts.15, s32[1,4,16]{2,1,0:T(4,128)} %rights.15, s32[1,4,16]{2,1,0:T(4,128)} %kinds.15, ...), custom_call_target="tpu_custom_call", output_to_operand_aliasing={{0}: (5, {}), {1}: (6, {}), {2}: (7, {}), {3}: (9, {})} | custom-call | flops 4000000000 | bytes 2097152 | tf_op jit(solution)/shard_map/pallas_call | solution.py:360
  35.8 3.9 %collective-permute-start.2 = (f32[1032,256]{1,0:T(8,128)}, f32[1032,256]{1,0:T(8,128)S(1)}, u32[]{:S(2)}, u32[]{:S(2)}) collective-permute-start(f32[1032,256]{1,0:T(8,128)} %get-tuple-element.53), channel_id=1, source_target_pairs={{0,1},{1,2},{2,3},{3,4},{4,5},{5,6},{6,7},{7,8},{8,9},{9,10},{10,1... | collective-permute-start | bytes 3170312 | tf_op jit(solution)/shard_map/ppermute | solution.py:424
  39.7 2.7 %collective-permute-done.3.refs_1_ = f32[1032,256]{1,0:T(8,128)S(1)} collective-permute-done((f32[1032,256]{1,0:T(8,128)}, f32[1032,256]{1,0:T(8,128)S(1)}, u32[]{:S(2)}, u32[]{:S(2)}) %collective-permute-start.3) | collective-permute-done | bytes 1056800 | tf_op jit(solution)/shard_map/ppermute | solution.py:424
  42.3 1.0 copy-done.6
  43.3 2.7 %shard_map.158 = (f32[1032,256]{1,0:T(8,128)}, f32[4,256,256]{2,1,0:T(8,128)}, f32[2048,256]{1,0:T(8,128)}) custom-call(s32[1,4,16]{2,1,0:T(4,128)} %lefts.15, s32[1,4,16]{2,1,0:T(4,128)} %rights.15, s32[1,4,16]{2,1,0:T(4,128)} %kinds.15, s32[1,4]{1,0:T(1,128)} %count.15, ...), custom_call_target="tpu_custom_call", output_to_operand_aliasing={{0}: (6, {}), {1}: (8, {})} | custom-call | flops 4000000000 | bytes 2097152 | tf_op jit(solution)/shard_map/pallas_call | solution.py:360
  46.0 6.2 %collective-permute-start.5 = (f32[1032,256]{1,0:T(8,128)}, f32[1032,256]{1,0:T(8,128)S(1)}, u32[]{:S(2)}, u32[]{:S(2)}) collective-permute-start(f32[1032,256]{1,0:T(8,128)} %get-tuple-element.61), channel_id=1, source_target_pairs={{0,1},{1,2},{2,3},{3,4},{4,5},{5,6},{6,7},{7,8},{8,9},{9,10},{10,1... | collective-permute-start | bytes 3170312 | tf_op jit(solution)/shard_map/ppermute | solution.py:424
  52.3 1.4 collective-permute-done.2.refs_2_
  53.7 1.0 copy-done.8
  54.7 5.2 %shard_map.159 = (f32[2048,256]{1,0:T(8,128)}, f32[16,128]{1,0:T(8,128)}, f32[1032,256]{1,0:T(8,128)}, f32[4,256,256]{2,1,0:T(8,128)}) custom-call(s32[1,4,16]{2,1,0:T(4,128)} %lefts.15, s32[1,4,16]{2,1,0:T(4,128)} %rights.15, s32[1,4,16]{2,1,0:T(4,128)} %kinds.15, ...), custom_call_target="tpu_custom_call", output_to_operand_aliasing={{0}: (5, {}), {1}: (6, {}), {2}: (7, {}), {3}: (9, {})} | custom-call | flops 4000000000 | bytes 2097152 | tf_op jit(solution)/shard_map/pallas_call | solution.py:360
  59.9 3.0 %collective-permute-start.4 = (f32[1032,256]{1,0:T(8,128)}, f32[1032,256]{1,0:T(8,128)S(1)}, u32[]{:S(2)}, u32[]{:S(2)}) collective-permute-start(f32[1032,256]{1,0:T(8,128)} %get-tuple-element.60), channel_id=1, source_target_pairs={{0,1},{1,2},{2,3},{3,4},{4,5},{5,6},{6,7},{7,8},{8,9},{9,10},{10,1... | collective-permute-start | bytes 3170312 | tf_op jit(solution)/shard_map/ppermute | solution.py:424
  62.8 2.2 %collective-permute-done.5.refs_1_ = f32[1032,256]{1,0:T(8,128)S(1)} collective-permute-done((f32[1032,256]{1,0:T(8,128)}, f32[1032,256]{1,0:T(8,128)S(1)}, u32[]{:S(2)}, u32[]{:S(2)}) %collective-permute-start.5) | collective-permute-done | bytes 1056800 | tf_op jit(solution)/shard_map/ppermute | solution.py:424
  65.0 1.0 copy-done.3
  66.0 6.3 %shard_map.160 = (f32[1032,256]{1,0:T(8,128)}, f32[4,256,256]{2,1,0:T(8,128)}, f32[2048,256]{1,0:T(8,128)}) custom-call(s32[1,4,16]{2,1,0:T(4,128)} %lefts.15, s32[1,4,16]{2,1,0:T(4,128)} %rights.15, s32[1,4,16]{2,1,0:T(4,128)} %kinds.15, s32[1,4]{1,0:T(1,128)} %count.15, ...), custom_call_target="tpu_custom_call", output_to_operand_aliasing={{0}: (6, {}), {1}: (8, {})} | custom-call | flops 4000000000 | bytes 2097152 | tf_op jit(solution)/shard_map/pallas_call | solution.py:360
  72.3 4.5 %collective-permute-start.7 = (f32[1032,256]{1,0:T(8,128)}, f32[1032,256]{1,0:T(8,128)S(1)}, u32[]{:S(2)}, u32[]{:S(2)}) collective-permute-start(f32[1032,256]{1,0:T(8,128)} %get-tuple-element.68), channel_id=1, source_target_pairs={{0,29},{1,30},{2,31},{3,0},{4,1},{5,2},{6,3},{7,4},{8,5},{9,6},{10... | collective-permute-start | bytes 3170312 | tf_op jit(solution)/shard_map/ppermute | solution.py:424
  76.8 1.0 copy-done.4
  77.8 7.6 %shard_map.161 = (f32[2048,256]{1,0:T(8,128)}, f32[16,128]{1,0:T(8,128)}, f32[1032,256]{1,0:T(8,128)}, f32[4,256,256]{2,1,0:T(8,128)}) custom-call(s32[1,4,16]{2,1,0:T(4,128)} %lefts.15, s32[1,4,16]{2,1,0:T(4,128)} %rights.15, s32[1,4,16]{2,1,0:T(4,128)} %kinds.15, ...), custom_call_target="tpu_custom_call", output_to_operand_aliasing={{0}: (5, {}), {1}: (6, {}), {2}: (7, {}), {3}: (9, {})} | custom-call | flops 4000000000 | bytes 2097152 | tf_op jit(solution)/shard_map/pallas_call | solution.py:360
  85.4 0.0 copy-start.1
  85.4 1.2 dynamic-slice_bitcast_fusion
  86.6 9.7 %collective-permute-start.6 = (f32[512,256]{1,0:T(8,128)S(1)}, f32[512,256]{1,0:T(8,128)S(1)}, u32[]{:S(2)}, u32[]{:S(2)}) collective-permute-start(f32[512,256]{1,0:T(8,128)S(1)} %dynamic-slice_bitcast_fusion), channel_id=1, source_target_pairs={{0,1},{1,0},{2,3},{3,2},{4,5},{5,4},{6,7},{7,6},{8,9},{9,8},{10,11... | collective-permute-start | bytes 1572872 | tf_op jit(solution)/shard_map/ppermute | solution.py:455
  96.2 1.5 collective-permute-done.6
  97.8 0.1 bitcast_add_fusion
  97.9 0.5 collective-permute-done.7.refs_0_
  98.4 10.4 %collective-permute-start.10 = (f32[128,256]{1,0:T(8,128)S(1)}, f32[128,256]{1,0:T(8,128)S(1)}, u32[]{:S(2)}, u32[]{:S(2)}) collective-permute-start(f32[128,256]{1,0:T(8,128)S(1)} %get-tuple-element.85), channel_id=1, source_target_pairs={{0,6},{1,7},{2,4},{3,5},{4,2},{5,3},{6,0},{7,1},{8,14},{9,15},{10,... | collective-permute-start | bytes 393224 | tf_op jit(solution)/shard_map/ppermute | solution.py:455
  108.8 0.4 collective-permute-start.9
  109.2 2.0 %collective-permute-done.10 = f32[128,256]{1,0:T(8,128)S(1)} collective-permute-done((f32[128,256]{1,0:T(8,128)S(1)}, f32[128,256]{1,0:T(8,128)S(1)}, u32[]{:S(2)}, u32[]{:S(2)}) %collective-permute-start.10) | collective-permute-done | bytes 131104 | tf_op jit(solution)/shard_map/ppermute | solution.py:455
  111.2 1.5 collective-permute-done.8
  112.7 1.0 collective-permute-start.17
  113.7 3.7 %collective-permute-start.11 = (f32[32,256]{1,0:T(8,128)S(1)}, f32[32,256]{1,0:T(8,128)S(1)}, u32[]{:S(2)}, u32[]{:S(2)}) collective-permute-start(f32[32,256]{1,0:T(8,128)S(1)} %get-tuple-element.87), channel_id=1, source_target_pairs={{0,8},{1,9},{2,10},{3,11},{4,12},{5,13},{6,14},{7,15},{8,0},{9,1},... | collective-permute-start | bytes 98312 | tf_op jit(solution)/shard_map/ppermute | solution.py:455
  117.4 3.4 %collective-permute-start.12 = (f32[32,256]{1,0:T(8,128)S(1)}, f32[32,256]{1,0:T(8,128)S(1)}, u32[]{:S(2)}, u32[]{:S(2)}) collective-permute-start(f32[32,256]{1,0:T(8,128)S(1)} %get-tuple-element.89), channel_id=1, source_target_pairs={{0,16},{1,17},{2,18},{3,19},{4,20},{5,21},{6,22},{7,23},{8,24},{9,... | collective-permute-start | bytes 98312 | tf_op jit(solution)/shard_map/ppermute | solution.py:455
  120.7 0.2 collective-permute-start.13
  121.0 19.7 %collective-permute-done.11 = f32[32,256]{1,0:T(8,128)S(1)} collective-permute-done((f32[32,256]{1,0:T(8,128)S(1)}, f32[32,256]{1,0:T(8,128)S(1)}, u32[]{:S(2)}, u32[]{:S(2)}) %collective-permute-start.11) | collective-permute-done | bytes 32800 | tf_op jit(solution)/shard_map/ppermute | solution.py:455
  140.6 5.2 %collective-permute-done.12 = f32[32,256]{1,0:T(8,128)S(1)} collective-permute-done((f32[32,256]{1,0:T(8,128)S(1)}, f32[32,256]{1,0:T(8,128)S(1)}, u32[]{:S(2)}, u32[]{:S(2)}) %collective-permute-start.12) | collective-permute-done | bytes 32800 | tf_op jit(solution)/shard_map/ppermute | solution.py:455
  145.9 1.3 collective-permute-done.13
  147.3 0.4 collective-permute-start.14
  147.6 0.0 collective-permute-start.15
  147.6 2.3 %collective-permute-start.16 = (f32[32,256]{1,0:T(8,128)S(1)}, f32[32,256]{1,0:T(8,128)S(1)}, u32[]{:S(2)}, u32[]{:S(2)}) collective-permute-start(f32[32,256]{1,0:T(8,128)S(1)} %get-tuple-element.81), channel_id=1, source_target_pairs={{0,24},{1,25},{2,26},{3,27},{4,28},{5,29},{6,30},{7,31},{8,16},{9,... | collective-permute-start | bytes 98312 | tf_op jit(solution)/shard_map/ppermute | solution.py:467
  150.0 0.1 collective-permute-done.14
  150.1 1.3 collective-permute-done.15
  151.4 1.4 collective-permute-done.16
  152.8 0.1 collective-permute-start.18
  152.9 0.1 collective-permute-start.19
  153.0 2.6 %collective-permute-start.20 = (f32[128,256]{1,0:T(8,128)S(1)}, f32[128,256]{1,0:T(8,128)S(1)}, u32[]{:S(2)}, u32[]{:S(2)}) collective-permute-start(f32[128,256]{1,0:T(8,128)S(1)} %bitcast.69), channel_id=1, source_target_pairs={{0,6},{1,7},{2,4},{3,5},{4,2},{5,3},{6,0},{7,1},{8,14},{9,15},{10,... | collective-permute-start | bytes 393224 | tf_op jit(solution)/shard_map/ppermute | solution.py:467
  155.6 1.1 collective-permute-done.18
  156.7 1.9 %collective-permute-done.19 = f32[128,256]{1,0:T(8,128)S(1)} collective-permute-done((f32[128,256]{1,0:T(8,128)S(1)}, f32[128,256]{1,0:T(8,128)S(1)}, u32[]{:S(2)}, u32[]{:S(2)}) %collective-permute-start.19) | collective-permute-done | bytes 131104 | tf_op jit(solution)/shard_map/ppermute | solution.py:467
  158.7 3.1 %collective-permute-start.21 = (f32[512,256]{1,0:T(8,128)S(1)}, f32[512,256]{1,0:T(8,128)S(1)}, u32[]{:S(2)}, u32[]{:S(2)}) collective-permute-start(f32[512,256]{1,0:T(8,128)S(1)} %bitcast.63), channel_id=1, source_target_pairs={{0,1},{1,0},{2,3},{3,2},{4,5},{5,4},{6,7},{7,6},{8,9},{9,8},{10,11... | collective-permute-start | bytes 1572872 | tf_op jit(solution)/shard_map/ppermute | solution.py:467
  161.8 1.4 shard_map.162
  163.2 0.1 broadcast_in_dim.48
  163.3 0.0 collective-permute-done.21
  163.4 0.0 copy-start.2
  163.4 0.0 copy-start
  163.4 0.2 multiply_reduce_fusion
  163.7 0.4 copy-done.2
  164.1 0.6 sqrt_add_fusion
  164.7 1.2 divide_subtract_fusion
  (32 shorter events, 0.3 us)
Async XLA Ops:
  5.7 14.0 %collective-permute-start.1 = (f32[1032,256]{1,0:T(8,128)}, f32[1032,256]{1,0:T(8,128)S(1)}, u32[]{:S(2)}, u32[]{:S(2)}) collective-permute-start(f32[1032,256]{1,0:T(8,128)} %get-tuple-element.47), channel_id=1, source_target_pairs={{0,1},{1,2},{2,3},{3,4},{4,5},{5,6},{6,7},{7,8},{8,9},{9,10},{10,1... | collective-permute-start | bytes 3170312 | tf_op jit(solution)/shard_map/ppermute | solution.py:424
  13.7 17.3 %collective-permute-start = (f32[1032,256]{1,0:T(8,128)}, f32[1032,256]{1,0:T(8,128)S(1)}, u32[]{:S(2)}, u32[]{:S(2)}) collective-permute-start(f32[1032,256]{1,0:T(8,128)} %get-tuple-element.46), channel_id=1, source_target_pairs={{0,1},{1,2},{2,3},{3,4},{4,5},{5,6},{6,7},{7,8},{8,9},{9,10},{10,1... | collective-permute-start | bytes 3170312 | tf_op jit(solution)/shard_map/ppermute | solution.py:424
  19.7 1.0 copy-start.9
  27.2 15.2 %collective-permute-start.3 = (f32[1032,256]{1,0:T(8,128)}, f32[1032,256]{1,0:T(8,128)S(1)}, u32[]{:S(2)}, u32[]{:S(2)}) collective-permute-start(f32[1032,256]{1,0:T(8,128)} %get-tuple-element.54), channel_id=1, source_target_pairs={{0,1},{1,2},{2,3},{3,4},{4,5},{5,6},{6,7},{7,8},{8,9},{9,10},{10,1... | collective-permute-start | bytes 3170312 | tf_op jit(solution)/shard_map/ppermute | solution.py:424
  31.0 1.0 copy-start.7
  35.8 17.9 %collective-permute-start.2 = (f32[1032,256]{1,0:T(8,128)}, f32[1032,256]{1,0:T(8,128)S(1)}, u32[]{:S(2)}, u32[]{:S(2)}) collective-permute-start(f32[1032,256]{1,0:T(8,128)} %get-tuple-element.53), channel_id=1, source_target_pairs={{0,1},{1,2},{2,3},{3,4},{4,5},{5,6},{6,7},{7,8},{8,9},{9,10},{10,1... | collective-permute-start | bytes 3170312 | tf_op jit(solution)/shard_map/ppermute | solution.py:424
  42.3 1.0 copy-start.6
  46.0 18.9 %collective-permute-start.5 = (f32[1032,256]{1,0:T(8,128)}, f32[1032,256]{1,0:T(8,128)S(1)}, u32[]{:S(2)}, u32[]{:S(2)}) collective-permute-start(f32[1032,256]{1,0:T(8,128)} %get-tuple-element.61), channel_id=1, source_target_pairs={{0,1},{1,2},{2,3},{3,4},{4,5},{5,6},{6,7},{7,8},{8,9},{9,10},{10,1... | collective-permute-start | bytes 3170312 | tf_op jit(solution)/shard_map/ppermute | solution.py:424
  53.7 1.0 copy-start.8
  59.9 16.9 %collective-permute-start.4 = (f32[1032,256]{1,0:T(8,128)}, f32[1032,256]{1,0:T(8,128)S(1)}, u32[]{:S(2)}, u32[]{:S(2)}) collective-permute-start(f32[1032,256]{1,0:T(8,128)} %get-tuple-element.60), channel_id=1, source_target_pairs={{0,1},{1,2},{2,3},{3,4},{4,5},{5,6},{6,7},{7,8},{8,9},{9,10},{10,1... | collective-permute-start | bytes 3170312 | tf_op jit(solution)/shard_map/ppermute | solution.py:424
  65.0 1.0 copy-start.3
  72.3 26.1 %collective-permute-start.7 = (f32[1032,256]{1,0:T(8,128)}, f32[1032,256]{1,0:T(8,128)S(1)}, u32[]{:S(2)}, u32[]{:S(2)}) collective-permute-start(f32[1032,256]{1,0:T(8,128)} %get-tuple-element.68), channel_id=1, source_target_pairs={{0,29},{1,30},{2,31},{3,0},{4,1},{5,2},{6,3},{7,4},{8,5},{9,6},{10... | collective-permute-start | bytes 3170312 | tf_op jit(solution)/shard_map/ppermute | solution.py:424
  76.8 1.0 copy-start.4
  85.4 12.4 %copy-start.1 = (f32[4,256,256]{2,1,0:T(8,128)S(1)}, f32[4,256,256]{2,1,0:T(8,128)}, u32[]{:S(2)}) copy-start(f32[4,256,256]{2,1,0:T(8,128)} %get-tuple-element.67) | copy-start | bytes 3145732
  86.6 11.2 %collective-permute-start.6 = (f32[512,256]{1,0:T(8,128)S(1)}, f32[512,256]{1,0:T(8,128)S(1)}, u32[]{:S(2)}, u32[]{:S(2)}) collective-permute-start(f32[512,256]{1,0:T(8,128)S(1)} %dynamic-slice_bitcast_fusion), channel_id=1, source_target_pairs={{0,1},{1,0},{2,3},{3,2},{4,5},{5,4},{6,7},{7,6},{8,9},{9,8},{10,11... | collective-permute-start | bytes 1572872 | tf_op jit(solution)/shard_map/ppermute | solution.py:455
  97.8 14.8 %copy-start.5 = (f32[1032,256]{1,0:T(8,128)S(1)}, f32[1032,256]{1,0:T(8,128)}, u32[]{:S(2)}) copy-start(f32[1032,256]{1,0:T(8,128)} %get-tuple-element.73) | copy-start | bytes 3170308
  98.4 12.8 %collective-permute-start.10 = (f32[128,256]{1,0:T(8,128)S(1)}, f32[128,256]{1,0:T(8,128)S(1)}, u32[]{:S(2)}, u32[]{:S(2)}) collective-permute-start(f32[128,256]{1,0:T(8,128)S(1)} %get-tuple-element.85), channel_id=1, source_target_pairs={{0,6},{1,7},{2,4},{3,5},{4,2},{5,3},{6,0},{7,1},{8,14},{9,15},{10,... | collective-permute-start | bytes 393224 | tf_op jit(solution)/shard_map/ppermute | solution.py:455
  108.8 3.8 %collective-permute-start.8 = (f32[128,256]{1,0:T(8,128)S(1)}, f32[128,256]{1,0:T(8,128)S(1)}, u32[]{:S(2)}, u32[]{:S(2)}) collective-permute-start(f32[128,256]{1,0:T(8,128)S(1)} %get-tuple-element.84), channel_id=1, source_target_pairs={{0,2},{1,3},{2,0},{3,1},{4,6},{5,7},{6,4},{7,5},{8,10},{9,11},{10,... | collective-permute-start | bytes 393224 | tf_op jit(solution)/shard_map/ppermute | solution.py:455
  108.8 3.8 %collective-permute-start.9 = (f32[128,256]{1,0:T(8,128)S(1)}, f32[128,256]{1,0:T(8,128)S(1)}, u32[]{:S(2)}, u32[]{:S(2)}) collective-permute-start(f32[128,256]{1,0:T(8,128)S(1)} %get-tuple-element.86), channel_id=1, source_target_pairs={{0,4},{1,5},{2,6},{3,7},{4,0},{5,1},{6,2},{7,3},{8,12},{9,13},{10,... | collective-permute-start | bytes 393224 | tf_op jit(solution)/shard_map/ppermute | solution.py:455
  112.7 40.1 %collective-permute-start.17 = (f32[1032,256]{1,0:T(8,128)S(1)}, f32[1032,256]{1,0:T(8,128)S(1)}, u32[]{:S(2)}, u32[]{:S(2)}) collective-permute-start(f32[1032,256]{1,0:T(8,128)S(1)} %copy-done.5), channel_id=1, source_target_pairs={{0,29},{1,30},{2,31},{3,0},{4,1},{5,2},{6,3},{7,4},{8,5},{9,6},{10... | collective-permute-start | bytes 3170312 | tf_op jit(solution)/shard_map/ppermute | solution.py:424
  113.7 27.0 %collective-permute-start.11 = (f32[32,256]{1,0:T(8,128)S(1)}, f32[32,256]{1,0:T(8,128)S(1)}, u32[]{:S(2)}, u32[]{:S(2)}) collective-permute-start(f32[32,256]{1,0:T(8,128)S(1)} %get-tuple-element.87), channel_id=1, source_target_pairs={{0,8},{1,9},{2,10},{3,11},{4,12},{5,13},{6,14},{7,15},{8,0},{9,1},... | collective-permute-start | bytes 98312 | tf_op jit(solution)/shard_map/ppermute | solution.py:455
  117.4 28.5 %collective-permute-start.12 = (f32[32,256]{1,0:T(8,128)S(1)}, f32[32,256]{1,0:T(8,128)S(1)}, u32[]{:S(2)}, u32[]{:S(2)}) collective-permute-start(f32[32,256]{1,0:T(8,128)S(1)} %get-tuple-element.89), channel_id=1, source_target_pairs={{0,16},{1,17},{2,18},{3,19},{4,20},{5,21},{6,22},{7,23},{8,24},{9,... | collective-permute-start | bytes 98312 | tf_op jit(solution)/shard_map/ppermute | solution.py:455
  120.7 26.5 %collective-permute-start.13 = (f32[32,256]{1,0:T(8,128)S(1)}, f32[32,256]{1,0:T(8,128)S(1)}, u32[]{:S(2)}, u32[]{:S(2)}) collective-permute-start(f32[32,256]{1,0:T(8,128)S(1)} %get-tuple-element.88), channel_id=1, source_target_pairs={{0,24},{1,25},{2,26},{3,27},{4,28},{5,29},{6,30},{7,31},{8,16},{9,... | collective-permute-start | bytes 98312 | tf_op jit(solution)/shard_map/ppermute | solution.py:455
  147.3 2.8 %collective-permute-start.14 = (f32[32,256]{1,0:T(8,128)S(1)}, f32[32,256]{1,0:T(8,128)S(1)}, u32[]{:S(2)}, u32[]{:S(2)}) collective-permute-start(f32[32,256]{1,0:T(8,128)S(1)} %get-tuple-element.81), channel_id=1, source_target_pairs={{0,8},{1,9},{2,10},{3,11},{4,12},{5,13},{6,14},{7,15},{8,0},{9,1},... | collective-permute-start | bytes 98312 | tf_op jit(solution)/shard_map/ppermute | solution.py:467
  147.6 3.8 %collective-permute-start.15 = (f32[32,256]{1,0:T(8,128)S(1)}, f32[32,256]{1,0:T(8,128)S(1)}, u32[]{:S(2)}, u32[]{:S(2)}) collective-permute-start(f32[32,256]{1,0:T(8,128)S(1)} %get-tuple-element.81), channel_id=1, source_target_pairs={{0,16},{1,17},{2,18},{3,19},{4,20},{5,21},{6,22},{7,23},{8,24},{9,... | collective-permute-start | bytes 98312 | tf_op jit(solution)/shard_map/ppermute | solution.py:467
  147.6 5.2 %collective-permute-start.16 = (f32[32,256]{1,0:T(8,128)S(1)}, f32[32,256]{1,0:T(8,128)S(1)}, u32[]{:S(2)}, u32[]{:S(2)}) collective-permute-start(f32[32,256]{1,0:T(8,128)S(1)} %get-tuple-element.81), channel_id=1, source_target_pairs={{0,24},{1,25},{2,26},{3,27},{4,28},{5,29},{6,30},{7,31},{8,16},{9,... | collective-permute-start | bytes 98312 | tf_op jit(solution)/shard_map/ppermute | solution.py:467
  152.8 3.9 %collective-permute-start.18 = (f32[128,256]{1,0:T(8,128)S(1)}, f32[128,256]{1,0:T(8,128)S(1)}, u32[]{:S(2)}, u32[]{:S(2)}) collective-permute-start(f32[128,256]{1,0:T(8,128)S(1)} %bitcast.67), channel_id=1, source_target_pairs={{0,2},{1,3},{2,0},{3,1},{4,6},{5,7},{6,4},{7,5},{8,10},{9,11},{10,... | collective-permute-start | bytes 393224 | tf_op jit(solution)/shard_map/ppermute | solution.py:467
  152.9 5.7 %collective-permute-start.19 = (f32[128,256]{1,0:T(8,128)S(1)}, f32[128,256]{1,0:T(8,128)S(1)}, u32[]{:S(2)}, u32[]{:S(2)}) collective-permute-start(f32[128,256]{1,0:T(8,128)S(1)} %bitcast.68), channel_id=1, source_target_pairs={{0,4},{1,5},{2,6},{3,7},{4,0},{5,1},{6,2},{7,3},{8,12},{9,13},{10,... | collective-permute-start | bytes 393224 | tf_op jit(solution)/shard_map/ppermute | solution.py:467
  153.0 5.7 %collective-permute-start.20 = (f32[128,256]{1,0:T(8,128)S(1)}, f32[128,256]{1,0:T(8,128)S(1)}, u32[]{:S(2)}, u32[]{:S(2)}) collective-permute-start(f32[128,256]{1,0:T(8,128)S(1)} %bitcast.69), channel_id=1, source_target_pairs={{0,6},{1,7},{2,4},{3,5},{4,2},{5,3},{6,0},{7,1},{8,14},{9,15},{10,... | collective-permute-start | bytes 393224 | tf_op jit(solution)/shard_map/ppermute | solution.py:467
  158.7 4.7 %collective-permute-start.21 = (f32[512,256]{1,0:T(8,128)S(1)}, f32[512,256]{1,0:T(8,128)S(1)}, u32[]{:S(2)}, u32[]{:S(2)}) collective-permute-start(f32[512,256]{1,0:T(8,128)S(1)} %bitcast.63), channel_id=1, source_target_pairs={{0,1},{1,0},{2,3},{3,2},{4,5},{5,4},{6,7},{7,6},{8,9},{9,8},{10,11... | collective-permute-start | bytes 1572872 | tf_op jit(solution)/shard_map/ppermute | solution.py:467
  163.4 0.7 copy-start.2
  163.4 1.3 copy-start

commit v2 on v1

--- a/solution.py
+++ b/solution.py
@@ -14,8 +14,8 @@
 F32 = jnp.float32
 BF16 = jnp.bfloat16
 PARTS = 2
-TOGETHER = 2
-UPDATES = 4
+TOGETHER = 4
+UPDATES = 8
 
 NN = ((1,), (0,))
 NT = ((1,), (1,))
@@ -381,42 +381,40 @@
             dma((2, kinds_count)),
             dma((2,)),
         ],
-        compiler_params=pltpu.CompilerParams(vmem_limit_bytes=60 * 1024 * 1024),
+        compiler_params=pltpu.CompilerParams(vmem_limit_bytes=63 * 1024 * 1024),
         cost_estimate=pl.CostEstimate(flops=4 * 10**9, bytes_accessed=4 * left.size, transcendentals=0),
     )(*[value for _, value in names])
     return dict(zip([name for name, _ in outs], new))
 
 
-def unpack_kernel(*refs):
-    parts, (table, state), (sems,) = refs[:PARTS], refs[PARTS : PARTS + 2], refs[PARTS + 2 :]
+def unpack_kernel(layout, *refs):
+    pieces, (table, state), (sems,) = refs[: len(layout)], refs[len(layout) : len(layout) + 2], refs[len(layout) + 2 :]
     body = table.shape[0] // PARTS
     per_part, tile = state.shape[0] // PARTS, state.shape[1]
     copies = []
-    for n, part in enumerate(parts):
-        copies.append(
-            pltpu.make_async_copy(part.at[pl.ds(0, body)], table.at[pl.ds(n * body, body)], sems.at[2 * n])
-        )
-        copies.append(
-            pltpu.make_async_copy(
-                part.at[pl.ds(body, per_part), pl.ds(0, tile)], state.at[pl.ds(n * per_part, per_part)],
-                sems.at[2 * n + 1],
-            )
-        )
+    for (part, start, stop), piece in zip(layout, pieces):
+        rows = min(stop, body) - start
+        to = table.at[pl.ds(part * body + start, rows)]
+        copies.append(pltpu.make_async_copy(piece.at[pl.ds(0, rows)], to, sems.at[len(copies)]))
+        if stop > body:
+            of = piece.at[pl.ds(rows, per_part), pl.ds(0, tile)]
+            to = state.at[pl.ds(part * per_part, per_part)]
+            copies.append(pltpu.make_async_copy(of, to, sems.at[len(copies)]))
     for copy in copies:
         copy.start()
     for copy in copies:
         copy.wait()
 
 
-def unpack(parts, table, state):
+def unpack(layout, pieces, table, state):
     return pl.pallas_call(
-        unpack_kernel,
-        in_specs=[pl.BlockSpec(memory_space=pltpu.VMEM)] * PARTS,
+        functools.partial(unpack_kernel, layout),
+        in_specs=[pl.BlockSpec(memory_space=pltpu.VMEM)] * len(pieces),
         out_specs=[pl.BlockSpec(memory_space=pl.ANY)] * 2,
         out_shape=[jax.ShapeDtypeStruct(table, F32), jax.ShapeDtypeStruct(state, F32)],
-        scratch_shapes=[pltpu.SemaphoreType.DMA((2 * PARTS,))],
+        scratch_shapes=[pltpu.SemaphoreType.DMA((2 * len(pieces),))],
         compiler_params=pltpu.CompilerParams(vmem_limit_bytes=16 * 1024 * 1024),
-    )(*parts)
+    )(*pieces)
 
 
 def shifted(block, axis, distance):
@@ -436,7 +434,7 @@
         digits.append((at, 1 << wide))
         at += wide
     sends, arrived = list(sends), {0: shifted(sends[0], axis, distance)}
-    plan = iter([((), ()), ((), (0,)), ((1,), ()), ((), ()), ((), (1,))])
+    plan = iter([((), ()), ((1,), (0,)), ((2,), (1,)), ((), (2,))])
 
     def tie(block):
         send, want = next(plan, ((), ()))
@@ -447,24 +445,30 @@
             block, arrived[which] = lax.optimization_barrier((block, arrived[which]))
         return block
 
-    for at, size in digits:
+    def partners(at, size):
+        return [[(i, i ^ (j << at)) for i in range(n)] for j in range(1, size)]
+
+    *scattered, (last_at, last_size) = digits
+    for at, size in scattered:
         block = tie(block)
         mine = (me >> at) & (size - 1)
         parts = block.reshape(size, -1, block.shape[1])
         got = [
-            lax.ppermute(
-                lax.dynamic_index_in_dim(parts, mine ^ j, keepdims=False), axis,
-                [(i, i ^ (j << at)) for i in range(n)],
-            )
-            for j in range(1, size)
+            lax.ppermute(lax.dynamic_index_in_dim(parts, mine ^ j, keepdims=False), axis, route)
+            for j, route in enumerate(partners(at, size), 1)
         ]
         block = lax.dynamic_index_in_dim(parts, mine, keepdims=False)
         for other in got:
             block = block + other
-    for at, size in reversed(digits):
+    block = tie(block)
+    terms = [block] + [lax.ppermute(block, axis, route) for route in partners(last_at, last_size)]
+    while len(terms) > 1:
+        terms = [a + b for a, b in zip(terms[::2], terms[1::2])]
+    block = terms[0]
+    for at, size in reversed(scattered):
         block = tie(block)
         mine = (me >> at) & (size - 1)
-        got = [block] + [lax.ppermute(block, axis, [(i, i ^ (j << at)) for i in range(n)]) for j in range(1, size)]
+        got = [block] + [lax.ppermute(block, axis, route) for route in partners(at, size)]
         whole = jnp.zeros((size,) + block.shape, block.dtype)
         for j, other in enumerate(got):
             whole = lax.dynamic_update_index_in_dim(whole, other, mine ^ j, 0)
@@ -498,8 +502,12 @@
             rights_now[part] = shifted(new["right"], "dev", 1) if turn + 1 < rounds else new["right"]
         left, state_l = new["left"], new["state_l"]
     width = relations.shape[-1]
-    total, rights_now = sum_over(rel.reshape(-1, width), "dev", rights_now, 1 - rounds)
-    right, state_r = unpack(rights_now, right_table.shape, (right_state.shape[0] // tile, tile))
+    rows = rights_now[0].shape[0]
+    cut = rows // 2 // 8 * 8
+    cuts = [(0, 0, rows)] + [(1, start, stop) for start, stop in zip((0, cut), (cut, rows))]
+    pieces = [rights_now[0]] + [lax.slice_in_dim(rights_now[1], start, stop) for _, start, stop in cuts[1:]]
+    total, pieces = sum_over(rel.reshape(-1, width), "dev", pieces, 1 - rounds)
+    right, state_r = unpack(cuts, pieces, right_table.shape, (right_state.shape[0] // tile, tile))
     new_rel, new_state = adagrad_rows(relations.reshape(-1, width), relation_state.reshape(-1), total)
     return (
         left, state_l.reshape(left_state.shape), right, state_r.reshape(right_state.shape),

time: 169 us -> 164 us (0.970); the launches traced: 166 us -> 163 us
  Pallas kernels: 44.6 us -> 57.2 us
  waiting for transfers between devices: 51.8 us -> 41.9 us
  local copies, waits for them, and re-layouts: 7.84 us -> 4.04 us
    ppermute x7 -> x4, waiting for transfers between devices: 31.3 us -> 0.61 us  [sum_over(): lax.ppermute(lax.dynamic_index_in_dim(parts, mine ^ j, keepdims=False), a...]
    ppermute x7 -> x4, starting transfers between devices: 27.7 us -> 3.2 us  [sum_over(): lax.ppermute(lax.dynamic_index_in_dim(parts, mine ^ j, keepdims=False), a...]
    ppermute x8 -> x9, starting transfers between devices: 22.3 us -> 40 us  [shifted(): lax.ppermute(block, axis, [(i, (i + distance) % n) for i in range(n)])]
    ppermute x7, waiting for transfers between devices: 5.88 us -> 18.8 us  [sum_over(): lax.ppermute(block, axis, route)]
    pallas_call x8, Pallas kernels: 43.3 us -> 54.6 us  [run_part(): pl.pallas_call(functools.partial(bucket_kernel, turn, part, first, (tiles...]
    ppermute x8 -> x9, waiting for transfers between devices: 14.7 us -> 22.5 us  [shifted(): lax.ppermute(block, axis, [(i, (i + distance) % n) for i in range(n)])]
    unnamed x20 -> x6, local copies, waits for them, and re-layouts: 6.36 us -> 0.43 us
    ppermute x7, starting transfers between devices: 8.55 us -> 14 us  [sum_over(): lax.ppermute(block, axis, route)]
  transfers between devices with their start and end apart: 22 -> 20, of which waited for: 17 -> 13; matrix products, arithmetic and copies ran while one was open for 1% -> 2% of each run, Pallas kernels for 24% -> 30%
where the time goes in v2:
time: 164 us; the launch traced here: 163 us
  Pallas kernels  57.2 us (35%)
  starting transfers between devices  57.1 us (35%)
  waiting for transfers between devices  41.9 us (26%)
  local copies, waits for them, and re-layouts  4.04 us (2%)
  other arithmetic  2.14 us (1%)
    pallas_call x8, Pallas kernels, run_part(): pl.pallas_call(functools.partial(bucket_kernel, turn, part, first, (tiles...  54.6 us
    ppermute x9, starting transfers between devices, shifted(): lax.ppermute(block, axis, [(i, (i + distance) % n) for i in range(n)])  40 us
    ppermute x9, waiting for transfers between devices, shifted(): lax.ppermute(block, axis, [(i, (i + distance) % n) for i in range(n)])  22.5 us
    ppermute x7, waiting for transfers between devices, sum_over(): lax.ppermute(block, axis, route)  18.8 us
    ppermute x7, starting transfers between devices, sum_over(): lax.ppermute(block, axis, route)  14 us
  transfers between devices with their start and end apart: 20, of which 13 were waited for; matrix products, arithmetic and copies ran while one was open for 2% of the time, Pallas kernels for 30%

profile of v2, /device:TPU:17, one launch (start us, length us, event | category | flops | bytes accessed | tf_op | source)
XLA Modules:
  0.0 163.3 jit_solution(3827696100507277125)
XLA Ops:
  0.6 8.3 %shard_map.154 = (f32[1032,256]{1,0:T(8,128)}, f32[4,256,256]{2,1,0:T(8,128)}, f32[2048,256]{1,0:T(8,128)}) custom-call(s32[1,4,16]{2,1,0:T(4,128)} %lefts.15, s32[1,4,16]{2,1,0:T(4,128)} %rights.15, s32[1,4,16]{2,1,0:T(4,128)} %kinds.15, s32[1,4]{1,0:T(1,128)} %count.15, s32[1,4,16,128,128]{4,3,2,1,0:T(8,128)} %edges.15, f32[2048,256]{1,0:T(8,128)} %refs_0_.3, ...), custom_call_target="tpu_custom_call" | custom-call | flops 4000000000 | bytes 2097152 | tf_op jit(solution)/shard_map/pallas_call | solution.py:360
  9.0 0.1 collective-permute-start.1
  9.0 9.9 %shard_map.155 = (f32[2048,256]{1,0:T(8,128)}, f32[16,128]{1,0:T(8,128)}, f32[1032,256]{1,0:T(8,128)}, f32[4,256,256]{2,1,0:T(8,128)}) custom-call(s32[1,4,16]{2,1,0:T(4,128)} %lefts.15, s32[1,4,16]{2,1,0:T(4,128)} %rights.15, s32[1,4,16]{2,1,0:T(4,128)} %kinds.15, s32[1,4]{1,0:T(1,128)} %count.15, ...), custom_call_target="tpu_custom_call", output_to_operand_aliasing={{3}: (10, {})} | custom-call | flops 4000000000 | bytes 2097152 | tf_op jit(solution)/shard_map/pallas_call | solution.py:360
  18.9 0.1 collective-permute-start
  19.0 2.2 %collective-permute-done.1.refs_1_ = f32[1032,256]{1,0:T(8,128)} collective-permute-done((f32[1032,256]{1,0:T(8,128)}, f32[1032,256]{1,0:T(8,128)}, u32[]{:S(2)}, u32[]{:S(2)}) %collective-permute-start.1) | collective-permute-done | bytes 1056800 | tf_op jit(solution)/shard_map/ppermute | solution.py:422
  21.2 6.0 %shard_map.156 = (f32[1032,256]{1,0:T(8,128)}, f32[4,256,256]{2,1,0:T(8,128)}, f32[2048,256]{1,0:T(8,128)}) custom-call(s32[1,4,16]{2,1,0:T(4,128)} %lefts.15, s32[1,4,16]{2,1,0:T(4,128)} %rights.15, s32[1,4,16]{2,1,0:T(4,128)} %kinds.15, s32[1,4]{1,0:T(1,128)} %count.15, ...), custom_call_target="tpu_custom_call", output_to_operand_aliasing={{0}: (6, {}), {1}: (8, {})} | custom-call | flops 4000000000 | bytes 2097152 | tf_op jit(solution)/shard_map/pallas_call | solution.py:360
  27.1 4.9 %collective-permute-start.3 = (f32[1032,256]{1,0:T(8,128)}, f32[1032,256]{1,0:T(8,128)}, u32[]{:S(2)}, u32[]{:S(2)}) collective-permute-start(f32[1032,256]{1,0:T(8,128)} %get-tuple-element.58), channel_id=1, source_target_pairs={{0,1},{1,2},{2,3},{3,4},{4,5},{5,6},{6,7},{7,8},{8,9},{9,10},{10,1... | collective-permute-start | bytes 3170312 | tf_op jit(solution)/shard_map/ppermute | solution.py:422
  32.0 0.5 collective-permute-done.refs_2_
  32.5 6.1 %shard_map.157 = (f32[2048,256]{1,0:T(8,128)}, f32[16,128]{1,0:T(8,128)}, f32[1032,256]{1,0:T(8,128)}, f32[4,256,256]{2,1,0:T(8,128)}) custom-call(s32[1,4,16]{2,1,0:T(4,128)} %lefts.15, s32[1,4,16]{2,1,0:T(4,128)} %rights.15, s32[1,4,16]{2,1,0:T(4,128)} %kinds.15, ...), custom_call_target="tpu_custom_call", output_to_operand_aliasing={{0}: (5, {}), {1}: (6, {}), {2}: (7, {}), {3}: (9, {})} | custom-call | flops 4000000000 | bytes 2097152 | tf_op jit(solution)/shard_map/pallas_call | solution.py:360
  38.6 5.7 %collective-permute-start.2 = (f32[1032,256]{1,0:T(8,128)}, f32[1032,256]{1,0:T(8,128)}, u32[]{:S(2)}, u32[]{:S(2)}) collective-permute-start(f32[1032,256]{1,0:T(8,128)} %get-tuple-element.57), channel_id=1, source_target_pairs={{0,1},{1,2},{2,3},{3,4},{4,5},{5,6},{6,7},{7,8},{8,9},{9,10},{10,1... | collective-permute-start | bytes 3170312 | tf_op jit(solution)/shard_map/ppermute | solution.py:422
  44.4 0.0 collective-permute-done.3.refs_1_
  44.4 8.5 %shard_map.158 = (f32[1032,256]{1,0:T(8,128)}, f32[4,256,256]{2,1,0:T(8,128)}, f32[2048,256]{1,0:T(8,128)}) custom-call(s32[1,4,16]{2,1,0:T(4,128)} %lefts.15, s32[1,4,16]{2,1,0:T(4,128)} %rights.15, s32[1,4,16]{2,1,0:T(4,128)} %kinds.15, s32[1,4]{1,0:T(1,128)} %count.15, ...), custom_call_target="tpu_custom_call", output_to_operand_aliasing={{0}: (6, {}), {1}: (8, {})} | custom-call | flops 4000000000 | bytes 2097152 | tf_op jit(solution)/shard_map/pallas_call | solution.py:360
  52.9 0.1 collective-permute-start.5
  52.9 3.6 %collective-permute-done.2.refs_2_ = f32[1032,256]{1,0:T(8,128)} collective-permute-done((f32[1032,256]{1,0:T(8,128)}, f32[1032,256]{1,0:T(8,128)}, u32[]{:S(2)}, u32[]{:S(2)}) %collective-permute-start.2) | collective-permute-done | bytes 1056800 | tf_op jit(solution)/shard_map/ppermute | solution.py:422
  56.5 7.0 %shard_map.159 = (f32[2048,256]{1,0:T(8,128)}, f32[16,128]{1,0:T(8,128)}, f32[1032,256]{1,0:T(8,128)}, f32[4,256,256]{2,1,0:T(8,128)}) custom-call(s32[1,4,16]{2,1,0:T(4,128)} %lefts.15, s32[1,4,16]{2,1,0:T(4,128)} %rights.15, s32[1,4,16]{2,1,0:T(4,128)} %kinds.15, ...), custom_call_target="tpu_custom_call", output_to_operand_aliasing={{0}: (5, {}), {1}: (6, {}), {2}: (7, {}), {3}: (9, {})} | custom-call | flops 4000000000 | bytes 2097152 | tf_op jit(solution)/shard_map/pallas_call | solution.py:360
  63.6 1.7 %collective-permute-start.4 = (f32[1032,256]{1,0:T(8,128)}, f32[1032,256]{1,0:T(8,128)}, u32[]{:S(2)}, u32[]{:S(2)}) collective-permute-start(f32[1032,256]{1,0:T(8,128)} %get-tuple-element.64), channel_id=1, source_target_pairs={{0,1},{1,2},{2,3},{3,4},{4,5},{5,6},{6,7},{7,8},{8,9},{9,10},{10,1... | collective-permute-start | bytes 3170312 | tf_op jit(solution)/shard_map/ppermute | solution.py:422
  65.3 2.6 %collective-permute-done.5.refs_1_ = f32[1032,256]{1,0:T(8,128)} collective-permute-done((f32[1032,256]{1,0:T(8,128)}, f32[1032,256]{1,0:T(8,128)}, u32[]{:S(2)}, u32[]{:S(2)}) %collective-permute-start.5) | collective-permute-done | bytes 1056800 | tf_op jit(solution)/shard_map/ppermute | solution.py:422
  67.8 2.7 %shard_map.160 = (f32[1032,256]{1,0:T(8,128)}, f32[4,256,256]{2,1,0:T(8,128)}, f32[2048,256]{1,0:T(8,128)}) custom-call(s32[1,4,16]{2,1,0:T(4,128)} %lefts.15, s32[1,4,16]{2,1,0:T(4,128)} %rights.15, s32[1,4,16]{2,1,0:T(4,128)} %kinds.15, s32[1,4]{1,0:T(1,128)} %count.15, ...), custom_call_target="tpu_custom_call", output_to_operand_aliasing={{0}: (6, {}), {1}: (8, {})} | custom-call | flops 4000000000 | bytes 2097152 | tf_op jit(solution)/shard_map/pallas_call | solution.py:360
  70.6 6.9 %collective-permute-start.7 = (f32[1032,256]{1,0:T(8,128)}, f32[1032,256]{1,0:T(8,128)}, u32[]{:S(2)}, u32[]{:S(2)}) collective-permute-start(f32[1032,256]{1,0:T(8,128)} %get-tuple-element.74), channel_id=1, source_target_pairs={{0,29},{1,30},{2,31},{3,0},{4,1},{5,2},{6,3},{7,4},{8,5},{9,6},{10... | collective-permute-start | bytes 3170312 | tf_op jit(solution)/shard_map/ppermute | solution.py:422
  77.5 6.8 %collective-permute-done.4.refs_2_ = f32[1032,256]{1,0:T(8,128)} collective-permute-done((f32[1032,256]{1,0:T(8,128)}, f32[1032,256]{1,0:T(8,128)}, u32[]{:S(2)}, u32[]{:S(2)}) %collective-permute-start.4) | collective-permute-done | bytes 1056800 | tf_op jit(solution)/shard_map/ppermute | solution.py:422
  84.3 6.1 %shard_map.161 = (f32[2048,256]{1,0:T(8,128)}, f32[16,128]{1,0:T(8,128)}, f32[1032,256]{1,0:T(8,128)}, f32[4,256,256]{2,1,0:T(8,128)}) custom-call(s32[1,4,16]{2,1,0:T(4,128)} %lefts.15, s32[1,4,16]{2,1,0:T(4,128)} %rights.15, s32[1,4,16]{2,1,0:T(4,128)} %kinds.15, ...), custom_call_target="tpu_custom_call", output_to_operand_aliasing={{0}: (5, {}), {1}: (6, {}), {2}: (7, {}), {3}: (9, {})} | custom-call | flops 4000000000 | bytes 2097152 | tf_op jit(solution)/shard_map/pallas_call | solution.py:360
  90.3 0.0 copy-start.1
  90.3 1.2 dynamic-slice_bitcast_fusion
  91.5 0.5 collective-permute-start.6
  92.0 1.1 slice.6
  93.1 0.5 collective-permute-done.6
  93.5 0.0 copy-done.1
  93.5 0.1 bitcast_add_fusion
  93.6 6.9 %collective-permute-done.7.refs_0_ = f32[1032,256]{1,0:T(8,128)} collective-permute-done((f32[1032,256]{1,0:T(8,128)}, f32[1032,256]{1,0:T(8,128)}, u32[]{:S(2)}, u32[]{:S(2)}) %collective-permute-start.7) | collective-permute-done | bytes 1056800 | tf_op jit(solution)/shard_map/ppermute | solution.py:422
  100.5 1.9 %collective-permute-start.10 = (f32[128,256]{1,0:T(8,128)S(1)}, f32[128,256]{1,0:T(8,128)S(1)}, u32[]{:S(2)}, u32[]{:S(2)}) collective-permute-start(f32[128,256]{1,0:T(8,128)S(1)} %get-tuple-element.91), channel_id=1, source_target_pairs={{0,6},{1,7},{2,4},{3,5},{4,2},{5,3},{6,0},{7,1},{8,14},{9,15},{10,... | collective-permute-start | bytes 393224 | tf_op jit(solution)/shard_map/ppermute | solution.py:457
  102.4 0.2 collective-permute-start.8
  102.6 0.6 collective-permute-start.9
  103.3 5.1 %collective-permute-start.11 = (f32[512,256]{1,0:T(8,128)S(1)}, f32[512,256]{1,0:T(8,128)S(1)}, u32[]{:S(2)}, u32[]{:S(2)}) collective-permute-start(f32[512,256]{1,0:T(8,128)S(1)} %slice.6), channel_id=1, source_target_pairs={{0,29},{1,30},{2,31},{3,0},{4,1},{5,2},{6,3},{7,4},{8,5},{9,6},{10... | collective-permute-start | bytes 1572872 | tf_op jit(solution)/shard_map/ppermute | solution.py:422
  108.4 1.1 slice.7
  109.5 0.0 collective-permute-done.10
  109.5 0.0 collective-permute-done.8
  109.5 0.1 collective-permute-done.9
  109.7 15.4 %collective-permute-start.15 = (f32[520,256]{1,0:T(8,128)S(1)}, f32[520,256]{1,0:T(8,128)S(1)}, u32[]{:S(2)}, u32[]{:S(2)}) collective-permute-start(f32[520,256]{1,0:T(8,128)S(1)} %slice.7), channel_id=1, source_target_pairs={{0,29},{1,30},{2,31},{3,0},{4,1},{5,2},{6,3},{7,4},{8,5},{9,6},{10... | collective-permute-start | bytes 1597448 | tf_op jit(solution)/shard_map/ppermute | solution.py:422
  125.1 0.0 collective-permute-done.11.refs_1_
  125.1 0.0 collective-permute-start.12
  125.1 2.0 %collective-permute-start.13 = (f32[128,256]{1,0:T(8,128)S(1)}, f32[128,256]{1,0:T(8,128)S(1)}, u32[]{:S(2)}, u32[]{:S(2)}) collective-permute-start(f32[128,256]{1,0:T(8,128)S(1)} %fusion.1), channel_id=1, source_target_pairs={{0,16},{1,17},{2,18},{3,19},{4,20},{5,21},{6,22},{7,23},{8,24},{9,... | collective-permute-start | bytes 393224 | tf_op jit(solution)/shard_map/ppermute | solution.py:464
  127.1 0.7 collective-permute-start.14
  127.7 9.2 %collective-permute-done.12 = f32[128,256]{1,0:T(8,128)S(1)} collective-permute-done((f32[128,256]{1,0:T(8,128)S(1)}, f32[128,256]{1,0:T(8,128)S(1)}, u32[]{:S(2)}, u32[]{:S(2)}) %collective-permute-start.12) | collective-permute-done | bytes 131104 | tf_op jit(solution)/shard_map/ppermute | solution.py:464
  136.9 3.2 %collective-permute-done.13 = f32[128,256]{1,0:T(8,128)S(1)} collective-permute-done((f32[128,256]{1,0:T(8,128)S(1)}, f32[128,256]{1,0:T(8,128)S(1)}, u32[]{:S(2)}, u32[]{:S(2)}) %collective-permute-start.13) | collective-permute-done | bytes 131104 | tf_op jit(solution)/shard_map/ppermute | solution.py:464
  140.2 1.8 %collective-permute-done.14 = f32[128,256]{1,0:T(8,128)S(1)} collective-permute-done((f32[128,256]{1,0:T(8,128)S(1)}, f32[128,256]{1,0:T(8,128)S(1)}, u32[]{:S(2)}, u32[]{:S(2)}) %collective-permute-start.14) | collective-permute-done | bytes 131104 | tf_op jit(solution)/shard_map/ppermute | solution.py:464
  142.1 0.0 collective-permute-done.15.refs_2_
  142.1 7.1 %collective-permute-start.16 = (f32[128,256]{1,0:T(8,128)S(1)}, f32[128,256]{1,0:T(8,128)S(1)}, u32[]{:S(2)}, u32[]{:S(2)}) collective-permute-start(f32[128,256]{1,0:T(8,128)S(1)} %add_add_fusion), channel_id=1, source_target_pairs={{0,2},{1,3},{2,0},{3,1},{4,6},{5,7},{6,4},{7,5},{8,10},{9,11},{10,... | collective-permute-start | bytes 393224 | tf_op jit(solution)/shard_map/ppermute | solution.py:471
  149.2 0.0 collective-permute-start.17
  149.2 1.3 collective-permute-start.18
  150.5 1.0 collective-permute-done.16
  151.5 3.5 %collective-permute-done.17 = f32[128,256]{1,0:T(8,128)S(1)} collective-permute-done((f32[128,256]{1,0:T(8,128)S(1)}, f32[128,256]{1,0:T(8,128)S(1)}, u32[]{:S(2)}, u32[]{:S(2)}) %collective-permute-start.17) | collective-permute-done | bytes 131104 | tf_op jit(solution)/shard_map/ppermute | solution.py:471
  155.0 0.0 collective-permute-done.18
  155.0 3.0 %collective-permute-start.19 = (f32[512,256]{1,0:T(8,128)S(1)}, f32[512,256]{1,0:T(8,128)S(1)}, u32[]{:S(2)}, u32[]{:S(2)}) collective-permute-start(f32[512,256]{1,0:T(8,128)S(1)} %bitcast.40), channel_id=1, source_target_pairs={{0,1},{1,0},{2,3},{3,2},{4,5},{5,4},{6,7},{7,6},{8,9},{9,8},{10,11... | collective-permute-start | bytes 1572872 | tf_op jit(solution)/shard_map/ppermute | solution.py:471
  158.0 2.6 %shard_map.162 = (f32[2048,256]{1,0:T(8,128)}, f32[16,128]{1,0:T(8,128)}) custom-call(f32[1032,256]{1,0:T(8,128)} %collective-permute-done.7.refs_0_, f32[512,256]{1,0:T(8,128)S(1)} %collective-permute-done.11.refs_1_, f32[520,256]{1,0:T(8,128)S(1)} %collective-permute-done.15.refs_2_), custom_call_target="tpu_custom_call" | custom-call | tf_op jit(solution)/shard_map/pallas_call | solution.py:410
  160.6 0.1 broadcast_in_dim.27
  160.7 0.0 collective-permute-done.19
  160.8 0.0 copy-start.2
  160.8 0.0 copy-start
  160.8 0.2 multiply_reduce_fusion
  161.1 0.4 copy-done.2
  161.5 0.6 sqrt_add_fusion
  162.1 0.0 copy-done
  162.1 1.2 divide_subtract_fusion
  (12 shorter events, 0.3 us)
Async XLA Ops:
  9.0 12.2 %collective-permute-start.1 = (f32[1032,256]{1,0:T(8,128)}, f32[1032,256]{1,0:T(8,128)}, u32[]{:S(2)}, u32[]{:S(2)}) collective-permute-start(f32[1032,256]{1,0:T(8,128)} %get-tuple-element.51), channel_id=1, source_target_pairs={{0,1},{1,2},{2,3},{3,4},{4,5},{5,6},{6,7},{7,8},{8,9},{9,10},{10,1... | collective-permute-start | bytes 3170312 | tf_op jit(solution)/shard_map/ppermute | solution.py:422
  18.9 13.6 %collective-permute-start = (f32[1032,256]{1,0:T(8,128)}, f32[1032,256]{1,0:T(8,128)}, u32[]{:S(2)}, u32[]{:S(2)}) collective-permute-start(f32[1032,256]{1,0:T(8,128)} %get-tuple-element.50), channel_id=1, source_target_pairs={{0,1},{1,2},{2,3},{3,4},{4,5},{5,6},{6,7},{7,8},{8,9},{9,10},{10,1... | collective-permute-start | bytes 3170312 | tf_op jit(solution)/shard_map/ppermute | solution.py:422
  27.1 17.2 %collective-permute-start.3 = (f32[1032,256]{1,0:T(8,128)}, f32[1032,256]{1,0:T(8,128)}, u32[]{:S(2)}, u32[]{:S(2)}) collective-permute-start(f32[1032,256]{1,0:T(8,128)} %get-tuple-element.58), channel_id=1, source_target_pairs={{0,1},{1,2},{2,3},{3,4},{4,5},{5,6},{6,7},{7,8},{8,9},{9,10},{10,1... | collective-permute-start | bytes 3170312 | tf_op jit(solution)/shard_map/ppermute | solution.py:422
  38.6 17.9 %collective-permute-start.2 = (f32[1032,256]{1,0:T(8,128)}, f32[1032,256]{1,0:T(8,128)}, u32[]{:S(2)}, u32[]{:S(2)}) collective-permute-start(f32[1032,256]{1,0:T(8,128)} %get-tuple-element.57), channel_id=1, source_target_pairs={{0,1},{1,2},{2,3},{3,4},{4,5},{5,6},{6,7},{7,8},{8,9},{9,10},{10,1... | collective-permute-start | bytes 3170312 | tf_op jit(solution)/shard_map/ppermute | solution.py:422
  52.9 15.0 %collective-permute-start.5 = (f32[1032,256]{1,0:T(8,128)}, f32[1032,256]{1,0:T(8,128)}, u32[]{:S(2)}, u32[]{:S(2)}) collective-permute-start(f32[1032,256]{1,0:T(8,128)} %get-tuple-element.65), channel_id=1, source_target_pairs={{0,1},{1,2},{2,3},{3,4},{4,5},{5,6},{6,7},{7,8},{8,9},{9,10},{10,1... | collective-permute-start | bytes 3170312 | tf_op jit(solution)/shard_map/ppermute | solution.py:422
  63.6 20.7 %collective-permute-start.4 = (f32[1032,256]{1,0:T(8,128)}, f32[1032,256]{1,0:T(8,128)}, u32[]{:S(2)}, u32[]{:S(2)}) collective-permute-start(f32[1032,256]{1,0:T(8,128)} %get-tuple-element.64), channel_id=1, source_target_pairs={{0,1},{1,2},{2,3},{3,4},{4,5},{5,6},{6,7},{7,8},{8,9},{9,10},{10,1... | collective-permute-start | bytes 3170312 | tf_op jit(solution)/shard_map/ppermute | solution.py:422
  70.6 29.9 %collective-permute-start.7 = (f32[1032,256]{1,0:T(8,128)}, f32[1032,256]{1,0:T(8,128)}, u32[]{:S(2)}, u32[]{:S(2)}) collective-permute-start(f32[1032,256]{1,0:T(8,128)} %get-tuple-element.74), channel_id=1, source_target_pairs={{0,29},{1,30},{2,31},{3,0},{4,1},{5,2},{6,3},{7,4},{8,5},{9,6},{10... | collective-permute-start | bytes 3170312 | tf_op jit(solution)/shard_map/ppermute | solution.py:422
  90.3 3.2 %copy-start.1 = (f32[4,256,256]{2,1,0:T(8,128)S(1)}, f32[4,256,256]{2,1,0:T(8,128)}, u32[]{:S(2)}) copy-start(f32[4,256,256]{2,1,0:T(8,128)} %get-tuple-element.71) | copy-start | bytes 3145732
  91.5 2.0 %collective-permute-start.6 = (f32[512,256]{1,0:T(8,128)S(1)}, f32[512,256]{1,0:T(8,128)S(1)}, u32[]{:S(2)}, u32[]{:S(2)}) collective-permute-start(f32[512,256]{1,0:T(8,128)S(1)} %dynamic-slice_bitcast_fusion), channel_id=1, source_target_pairs={{0,1},{1,0},{2,3},{3,2},{4,5},{5,4},{6,7},{7,6},{8,9},{9,8},{10,11... | collective-permute-start | bytes 1572872 | tf_op jit(solution)/shard_map/ppermute | solution.py:457
  100.5 8.9 %collective-permute-start.10 = (f32[128,256]{1,0:T(8,128)S(1)}, f32[128,256]{1,0:T(8,128)S(1)}, u32[]{:S(2)}, u32[]{:S(2)}) collective-permute-start(f32[128,256]{1,0:T(8,128)S(1)} %get-tuple-element.91), channel_id=1, source_target_pairs={{0,6},{1,7},{2,4},{3,5},{4,2},{5,3},{6,0},{7,1},{8,14},{9,15},{10,... | collective-permute-start | bytes 393224 | tf_op jit(solution)/shard_map/ppermute | solution.py:457
  102.4 7.1 %collective-permute-start.8 = (f32[128,256]{1,0:T(8,128)S(1)}, f32[128,256]{1,0:T(8,128)S(1)}, u32[]{:S(2)}, u32[]{:S(2)}) collective-permute-start(f32[128,256]{1,0:T(8,128)S(1)} %get-tuple-element.90), channel_id=1, source_target_pairs={{0,2},{1,3},{2,0},{3,1},{4,6},{5,7},{6,4},{7,5},{8,10},{9,11},{10,... | collective-permute-start | bytes 393224 | tf_op jit(solution)/shard_map/ppermute | solution.py:457
  102.6 7.0 %collective-permute-start.9 = (f32[128,256]{1,0:T(8,128)S(1)}, f32[128,256]{1,0:T(8,128)S(1)}, u32[]{:S(2)}, u32[]{:S(2)}) collective-permute-start(f32[128,256]{1,0:T(8,128)S(1)} %get-tuple-element.92), channel_id=1, source_target_pairs={{0,4},{1,5},{2,6},{3,7},{4,0},{5,1},{6,2},{7,3},{8,12},{9,13},{10,... | collective-permute-start | bytes 393224 | tf_op jit(solution)/shard_map/ppermute | solution.py:457
  103.3 21.8 %collective-permute-start.11 = (f32[512,256]{1,0:T(8,128)S(1)}, f32[512,256]{1,0:T(8,128)S(1)}, u32[]{:S(2)}, u32[]{:S(2)}) collective-permute-start(f32[512,256]{1,0:T(8,128)S(1)} %slice.6), channel_id=1, source_target_pairs={{0,29},{1,30},{2,31},{3,0},{4,1},{5,2},{6,3},{7,4},{8,5},{9,6},{10... | collective-permute-start | bytes 1572872 | tf_op jit(solution)/shard_map/ppermute | solution.py:422
  109.7 32.4 %collective-permute-start.15 = (f32[520,256]{1,0:T(8,128)S(1)}, f32[520,256]{1,0:T(8,128)S(1)}, u32[]{:S(2)}, u32[]{:S(2)}) collective-permute-start(f32[520,256]{1,0:T(8,128)S(1)} %slice.7), channel_id=1, source_target_pairs={{0,29},{1,30},{2,31},{3,0},{4,1},{5,2},{6,3},{7,4},{8,5},{9,6},{10... | collective-permute-start | bytes 1597448 | tf_op jit(solution)/shard_map/ppermute | solution.py:422
  125.1 11.9 %collective-permute-start.12 = (f32[128,256]{1,0:T(8,128)S(1)}, f32[128,256]{1,0:T(8,128)S(1)}, u32[]{:S(2)}, u32[]{:S(2)}) collective-permute-start(f32[128,256]{1,0:T(8,128)S(1)} %fusion.1), channel_id=1, source_target_pairs={{0,8},{1,9},{2,10},{3,11},{4,12},{5,13},{6,14},{7,15},{8,0},{9,1},... | collective-permute-start | bytes 393224 | tf_op jit(solution)/shard_map/ppermute | solution.py:464
  125.1 15.1 %collective-permute-start.13 = (f32[128,256]{1,0:T(8,128)S(1)}, f32[128,256]{1,0:T(8,128)S(1)}, u32[]{:S(2)}, u32[]{:S(2)}) collective-permute-start(f32[128,256]{1,0:T(8,128)S(1)} %fusion.1), channel_id=1, source_target_pairs={{0,16},{1,17},{2,18},{3,19},{4,20},{5,21},{6,22},{7,23},{8,24},{9,... | collective-permute-start | bytes 393224 | tf_op jit(solution)/shard_map/ppermute | solution.py:464
  127.1 15.0 %collective-permute-start.14 = (f32[128,256]{1,0:T(8,128)S(1)}, f32[128,256]{1,0:T(8,128)S(1)}, u32[]{:S(2)}, u32[]{:S(2)}) collective-permute-start(f32[128,256]{1,0:T(8,128)S(1)} %fusion.1), channel_id=1, source_target_pairs={{0,24},{1,25},{2,26},{3,27},{4,28},{5,29},{6,30},{7,31},{8,16},{9,... | collective-permute-start | bytes 393224 | tf_op jit(solution)/shard_map/ppermute | solution.py:464
  142.1 9.5 %collective-permute-start.16 = (f32[128,256]{1,0:T(8,128)S(1)}, f32[128,256]{1,0:T(8,128)S(1)}, u32[]{:S(2)}, u32[]{:S(2)}) collective-permute-start(f32[128,256]{1,0:T(8,128)S(1)} %add_add_fusion), channel_id=1, source_target_pairs={{0,2},{1,3},{2,0},{3,1},{4,6},{5,7},{6,4},{7,5},{8,10},{9,11},{10,... | collective-permute-start | bytes 393224 | tf_op jit(solution)/shard_map/ppermute | solution.py:471
  149.2 5.8 %collective-permute-start.17 = (f32[128,256]{1,0:T(8,128)S(1)}, f32[128,256]{1,0:T(8,128)S(1)}, u32[]{:S(2)}, u32[]{:S(2)}) collective-permute-start(f32[128,256]{1,0:T(8,128)S(1)} %add_add_fusion), channel_id=1, source_target_pairs={{0,4},{1,5},{2,6},{3,7},{4,0},{5,1},{6,2},{7,3},{8,12},{9,13},{10,... | collective-permute-start | bytes 393224 | tf_op jit(solution)/shard_map/ppermute | solution.py:471
  149.2 5.8 %collective-permute-start.18 = (f32[128,256]{1,0:T(8,128)S(1)}, f32[128,256]{1,0:T(8,128)S(1)}, u32[]{:S(2)}, u32[]{:S(2)}) collective-permute-start(f32[128,256]{1,0:T(8,128)S(1)} %add_add_fusion), channel_id=1, source_target_pairs={{0,6},{1,7},{2,4},{3,5},{4,2},{5,3},{6,0},{7,1},{8,14},{9,15},{10,... | collective-permute-start | bytes 393224 | tf_op jit(solution)/shard_map/ppermute | solution.py:471
  155.0 5.7 %collective-permute-start.19 = (f32[512,256]{1,0:T(8,128)S(1)}, f32[512,256]{1,0:T(8,128)S(1)}, u32[]{:S(2)}, u32[]{:S(2)}) collective-permute-start(f32[512,256]{1,0:T(8,128)S(1)} %bitcast.40), channel_id=1, source_target_pairs={{0,1},{1,0},{2,3},{3,2},{4,5},{5,4},{6,7},{7,6},{8,9},{9,8},{10,11... | collective-permute-start | bytes 1572872 | tf_op jit(solution)/shard_map/ppermute | solution.py:471
  160.8 0.7 copy-start.2
  160.8 1.3 copy-start

commit v3 on v2

--- a/solution.py
+++ b/solution.py
@@ -14,6 +14,7 @@
 F32 = jnp.float32
 BF16 = jnp.bfloat16
 PARTS = 2
+WAYS = ((0, 1), (0,), (1,))
 TOGETHER = 4
 UPDATES = 8
 
@@ -387,46 +388,53 @@
     return dict(zip([name for name, _ in outs], new))
 
 
-def unpack_kernel(layout, *refs):
-    pieces, (table, state), (sems,) = refs[: len(layout)], refs[len(layout) : len(layout) + 2], refs[len(layout) + 2 :]
+def unpack_kernel(turn, *refs):
+    pieces, (table, state), (sems,) = refs[: PARTS + 1], refs[PARTS + 1 : PARTS + 3], refs[PARTS + 3 :]
     body = table.shape[0] // PARTS
     per_part, tile = state.shape[0] // PARTS, state.shape[1]
-    copies = []
-    for (part, start, stop), piece in zip(layout, pieces):
-        rows = min(stop, body) - start
-        to = table.at[pl.ds(part * body + start, rows)]
-        copies.append(pltpu.make_async_copy(piece.at[pl.ds(0, rows)], to, sems.at[len(copies)]))
-        if stop > body:
-            of = piece.at[pl.ds(rows, per_part), pl.ds(0, tile)]
-            to = state.at[pl.ds(part * per_part, per_part)]
-            copies.append(pltpu.make_async_copy(of, to, sems.at[len(copies)]))
-    for copy in copies:
-        copy.start()
-    for copy in copies:
-        copy.wait()
-
-
-def unpack(layout, pieces, table, state):
+
+    def copies(part, piece):
+        states = piece.at[pl.ds(body, per_part), pl.ds(0, tile)]
+        return (
+            pltpu.make_async_copy(piece.at[pl.ds(0, body)], table.at[pl.ds(part * body, body)], sems.at[2 * part]),
+            pltpu.make_async_copy(states, state.at[pl.ds(part * per_part, per_part)], sems.at[2 * part + 1]),
+        )
+
+    def each(act):
+        for part in range(PARTS - 1):
+            for copy in copies(part, pieces[part]):
+                act(copy)
+        for way in (0, 1):
+            @pl.when(turn[0] == way)
+            def _():
+                for copy in copies(PARTS - 1, pieces[PARTS - 1 + way]):
+                    act(copy)
+
+    each(lambda copy: copy.start())
+    each(lambda copy: copy.wait())
+
+
+def unpack(turn, pieces, table, state):
     return pl.pallas_call(
-        functools.partial(unpack_kernel, layout),
-        in_specs=[pl.BlockSpec(memory_space=pltpu.VMEM)] * len(pieces),
+        unpack_kernel,
+        in_specs=[pl.BlockSpec(memory_space=pltpu.SMEM)] + [pl.BlockSpec(memory_space=pltpu.VMEM)] * len(pieces),
         out_specs=[pl.BlockSpec(memory_space=pl.ANY)] * 2,
         out_shape=[jax.ShapeDtypeStruct(table, F32), jax.ShapeDtypeStruct(state, F32)],
-        scratch_shapes=[pltpu.SemaphoreType.DMA((2 * len(pieces),))],
+        scratch_shapes=[pltpu.SemaphoreType.DMA((2 * PARTS,))],
         compiler_params=pltpu.CompilerParams(vmem_limit_bytes=16 * 1024 * 1024),
-    )(*pieces)
-
-
-def shifted(block, axis, distance):
+    )(turn, *pieces)
+
+
+def shifted(block, axis, distance, senders=(0, 1)):
     n = lax.axis_size(axis)
-    return lax.ppermute(block, axis, [(i, (i + distance) % n) for i in range(n)])
+    return lax.ppermute(block, axis, [(i, (i + distance) % n) for i in range(n) if i % 2 in senders])
 
 
 def sum_over(block, axis, sends, distance):
     n = lax.axis_size(axis)
     bits = n.bit_length() - 1
     if n != 1 << bits or block.shape[0] % n:
-        return lax.psum(block, axis), [shifted(x, axis, distance) for x in sends]
+        return lax.psum(block, axis), [shifted(x, axis, distance, way) for x, way in zip(sends, WAYS)]
     me = lax.axis_index(axis)
     digits, at = [], 0
     while at < bits:
@@ -434,13 +442,13 @@
         digits.append((at, 1 << wide))
         at += wide
     sends, arrived = list(sends), {0: shifted(sends[0], axis, distance)}
-    plan = iter([((), ()), ((1,), (0,)), ((2,), (1,)), ((), (2,))])
+    plan = iter([((), ()), ((1,), (0,)), ((2,), ()), ((), (1,)), ((), (2,))])
 
     def tie(block):
         send, want = next(plan, ((), ()))
         for which in send:
             block, sends[which] = lax.optimization_barrier((block, sends[which]))
-            arrived[which] = shifted(sends[which], axis, distance)
+            arrived[which] = shifted(sends[which], axis, distance, WAYS[which])
         for which in want:
             block, arrived[which] = lax.optimization_barrier((block, arrived[which]))
         return block
@@ -474,7 +482,7 @@
             whole = lax.dynamic_update_index_in_dim(whole, other, mine ^ j, 0)
         block = whole.reshape(-1, block.shape[1])
     tie(block)
-    return block, [arrived.get(i) if i in arrived else shifted(x, axis, distance) for i, x in enumerate(sends)]
+    return block, [arrived.get(i) if i in arrived else shifted(x, axis, distance, WAYS[i]) for i, x in enumerate(sends)]
 
 
 def adagrad_rows(table, state, grad):
@@ -502,12 +510,10 @@
             rights_now[part] = shifted(new["right"], "dev", 1) if turn + 1 < rounds else new["right"]
         left, state_l = new["left"], new["state_l"]
     width = relations.shape[-1]
-    rows = rights_now[0].shape[0]
-    cut = rows // 2 // 8 * 8
-    cuts = [(0, 0, rows)] + [(1, start, stop) for start, stop in zip((0, cut), (cut, rows))]
-    pieces = [rights_now[0]] + [lax.slice_in_dim(rights_now[1], start, stop) for _, start, stop in cuts[1:]]
-    total, pieces = sum_over(rel.reshape(-1, width), "dev", pieces, 1 - rounds)
-    right, state_r = unpack(cuts, pieces, right_table.shape, (right_state.shape[0] // tile, tile))
+    sends = [rights_now[0], rights_now[1], rights_now[1]]
+    total, pieces = sum_over(rel.reshape(-1, width), "dev", sends, 1 - rounds)
+    way = lax.rem(lax.axis_index("dev") + rounds - 1, 2).reshape(1)
+    right, state_r = unpack(way, pieces, right_table.shape, (right_state.shape[0] // tile, tile))
     new_rel, new_state = adagrad_rows(relations.reshape(-1, width), relation_state.reshape(-1), total)
     return (
         left, state_l.reshape(left_state.shape), right, state_r.reshape(right_state.shape),

time: 164 us -> 163 us (level)
  waiting for transfers between devices: 41.9 us -> 60.7 us
  starting transfers between devices: 57.1 us -> 45.3 us
  Pallas kernels: 57.2 us -> 51.7 us
  local copies, waits for them, and re-layouts: 4.04 us -> 1.88 us
    ppermute x9, starting transfers between devices: 40 us -> 22.8 us  [shifted(): lax.ppermute(block, axis, [(i, (i + distance) % n) for i in range(n) if i...]
    ppermute x4, waiting for transfers between devices: 0.61 us -> 13.2 us  [sum_over(): lax.ppermute(lax.dynamic_index_in_dim(parts, mine ^ j, keepdims=False), a...]
    ppermute x4, starting transfers between devices: 3.2 us -> 9.04 us  [sum_over(): lax.ppermute(lax.dynamic_index_in_dim(parts, mine ^ j, keepdims=False), a...]
    pallas_call x8, Pallas kernels: 54.6 us -> 49.1 us  [run_part(): pl.pallas_call(functools.partial(bucket_kernel, turn, part, first, (tiles...]
    ppermute x7, waiting for transfers between devices: 18.8 us -> 23.8 us  [sum_over(): lax.ppermute(block, axis, route)]
    slice x2 -> x0, local copies, waits for them, and re-layouts: 2.15 us -> none  [per_device(): lax.slice_in_dim(rights_now[1], start, stop)]
  transfers between devices with their start and end apart: 20 -> 20, of which waited for: 13 -> 15; matrix products, arithmetic and copies ran while one was open for 2% -> 1% of each run, Pallas kernels for 30% -> 28%
where the time goes in v3:
time: 163 us
  waiting for transfers between devices  60.7 us (37%)
  Pallas kernels  51.7 us (32%)
  starting transfers between devices  45.3 us (28%)
  other arithmetic  2.14 us (1%)
  local copies, waits for them, and re-layouts  1.88 us (1%)
    pallas_call x8, Pallas kernels, run_part(): pl.pallas_call(functools.partial(bucket_kernel, turn, part, first, (tiles...  49.1 us
    ppermute x7, waiting for transfers between devices, sum_over(): lax.ppermute(block, axis, route)  23.8 us
    ppermute x9, waiting for transfers between devices, shifted(): lax.ppermute(block, axis, [(i, (i + distance) % n) for i in range(n) if i...  23.7 us
    ppermute x9, starting transfers between devices, shifted(): lax.ppermute(block, axis, [(i, (i + distance) % n) for i in range(n) if i...  22.8 us
    ppermute x7, starting transfers between devices, sum_over(): lax.ppermute(block, axis, route)  13.4 us
    ppermute x4, waiting for transfers between devices, sum_over(): lax.ppermute(lax.dynamic_index_in_dim(parts, mine ^ j, keepdims=False), a...  13.2 us
    ppermute x4, starting transfers between devices, sum_over(): lax.ppermute(lax.dynamic_index_in_dim(parts, mine ^ j, keepdims=False), a...  9.04 us
  transfers between devices with their start and end apart: 20, of which 15 were waited for; matrix products, arithmetic and copies ran while one was open for 1% of the time, Pallas kernels for 28%

profile of v3, /device:TPU:17, one launch (start us, length us, event | category | flops | bytes accessed | tf_op | source)
XLA Modules:
  0.0 162.6 jit_solution(8385196165701712099)
XLA Ops:
  0.6 5.9 %shard_map.154 = (f32[1032,256]{1,0:T(8,128)}, f32[4,256,256]{2,1,0:T(8,128)}, f32[2048,256]{1,0:T(8,128)}) custom-call(s32[1,4,16]{2,1,0:T(4,128)} %lefts.15, s32[1,4,16]{2,1,0:T(4,128)} %rights.15, s32[1,4,16]{2,1,0:T(4,128)} %kinds.15, s32[1,4]{1,0:T(1,128)} %count.15, s32[1,4,16,128,128]{4,3,2,1,0:T(8,128)} %edges.15, f32[2048,256]{1,0:T(8,128)} %refs_0_.3, ...), custom_call_target="tpu_custom_call" | custom-call | flops 4000000000 | bytes 2097152 | tf_op jit(solution)/shard_map/pallas_call | solution.py:361
  6.6 4.1 %collective-permute-start.1 = (f32[1032,256]{1,0:T(8,128)}, f32[1032,256]{1,0:T(8,128)}, u32[]{:S(2)}, u32[]{:S(2)}) collective-permute-start(f32[1032,256]{1,0:T(8,128)} %get-tuple-element.51), channel_id=1, source_target_pairs={{0,1},{1,2},{2,3},{3,4},{4,5},{5,6},{6,7},{7,8},{8,9},{9,10},{10,1... | collective-permute-start | bytes 3170312 | tf_op jit(solution)/shard_map/ppermute | solution.py:430
  10.6 5.0 %shard_map.155 = (f32[2048,256]{1,0:T(8,128)}, f32[16,128]{1,0:T(8,128)}, f32[1032,256]{1,0:T(8,128)}, f32[4,256,256]{2,1,0:T(8,128)}) custom-call(s32[1,4,16]{2,1,0:T(4,128)} %lefts.15, s32[1,4,16]{2,1,0:T(4,128)} %rights.15, s32[1,4,16]{2,1,0:T(4,128)} %kinds.15, s32[1,4]{1,0:T(1,128)} %count.15, ...), custom_call_target="tpu_custom_call", output_to_operand_aliasing={{3}: (10, {})} | custom-call | flops 4000000000 | bytes 2097152 | tf_op jit(solution)/shard_map/pallas_call | solution.py:361
  15.7 2.6 %collective-permute-start = (f32[1032,256]{1,0:T(8,128)}, f32[1032,256]{1,0:T(8,128)}, u32[]{:S(2)}, u32[]{:S(2)}) collective-permute-start(f32[1032,256]{1,0:T(8,128)} %get-tuple-element.50), channel_id=1, source_target_pairs={{0,1},{1,2},{2,3},{3,4},{4,5},{5,6},{6,7},{7,8},{8,9},{9,10},{10,1... | collective-permute-start | bytes 3170312 | tf_op jit(solution)/shard_map/ppermute | solution.py:430
  18.2 4.6 %collective-permute-done.1.refs_1_ = f32[1032,256]{1,0:T(8,128)} collective-permute-done((f32[1032,256]{1,0:T(8,128)}, f32[1032,256]{1,0:T(8,128)}, u32[]{:S(2)}, u32[]{:S(2)}) %collective-permute-start.1) | collective-permute-done | bytes 1056800 | tf_op jit(solution)/shard_map/ppermute | solution.py:430
  22.8 5.9 %shard_map.156 = (f32[1032,256]{1,0:T(8,128)}, f32[4,256,256]{2,1,0:T(8,128)}, f32[2048,256]{1,0:T(8,128)}) custom-call(s32[1,4,16]{2,1,0:T(4,128)} %lefts.15, s32[1,4,16]{2,1,0:T(4,128)} %rights.15, s32[1,4,16]{2,1,0:T(4,128)} %kinds.15, s32[1,4]{1,0:T(1,128)} %count.15, ...), custom_call_target="tpu_custom_call", output_to_operand_aliasing={{0}: (6, {}), {1}: (8, {})} | custom-call | flops 4000000000 | bytes 2097152 | tf_op jit(solution)/shard_map/pallas_call | solution.py:361
  28.7 2.6 %collective-permute-start.3 = (f32[1032,256]{1,0:T(8,128)}, f32[1032,256]{1,0:T(8,128)}, u32[]{:S(2)}, u32[]{:S(2)}) collective-permute-start(f32[1032,256]{1,0:T(8,128)} %get-tuple-element.58), channel_id=1, source_target_pairs={{0,1},{1,2},{2,3},{3,4},{4,5},{5,6},{6,7},{7,8},{8,9},{9,10},{10,1... | collective-permute-start | bytes 3170312 | tf_op jit(solution)/shard_map/ppermute | solution.py:430
  31.2 2.9 %collective-permute-done.refs_2_ = f32[1032,256]{1,0:T(8,128)} collective-permute-done((f32[1032,256]{1,0:T(8,128)}, f32[1032,256]{1,0:T(8,128)}, u32[]{:S(2)}, u32[]{:S(2)}) %collective-permute-start) | collective-permute-done | bytes 1056800 | tf_op jit(solution)/shard_map/ppermute | solution.py:430
  34.1 6.3 %shard_map.157 = (f32[2048,256]{1,0:T(8,128)}, f32[16,128]{1,0:T(8,128)}, f32[1032,256]{1,0:T(8,128)}, f32[4,256,256]{2,1,0:T(8,128)}) custom-call(s32[1,4,16]{2,1,0:T(4,128)} %lefts.15, s32[1,4,16]{2,1,0:T(4,128)} %rights.15, s32[1,4,16]{2,1,0:T(4,128)} %kinds.15, ...), custom_call_target="tpu_custom_call", output_to_operand_aliasing={{0}: (5, {}), {1}: (6, {}), {2}: (7, {}), {3}: (9, {})} | custom-call | flops 4000000000 | bytes 2097152 | tf_op jit(solution)/shard_map/pallas_call | solution.py:361
  40.4 2.3 %collective-permute-start.2 = (f32[1032,256]{1,0:T(8,128)}, f32[1032,256]{1,0:T(8,128)}, u32[]{:S(2)}, u32[]{:S(2)}) collective-permute-start(f32[1032,256]{1,0:T(8,128)} %get-tuple-element.57), channel_id=1, source_target_pairs={{0,1},{1,2},{2,3},{3,4},{4,5},{5,6},{6,7},{7,8},{8,9},{9,10},{10,1... | collective-permute-start | bytes 3170312 | tf_op jit(solution)/shard_map/ppermute | solution.py:430
  42.7 2.7 %collective-permute-done.3.refs_1_ = f32[1032,256]{1,0:T(8,128)} collective-permute-done((f32[1032,256]{1,0:T(8,128)}, f32[1032,256]{1,0:T(8,128)}, u32[]{:S(2)}, u32[]{:S(2)}) %collective-permute-start.3) | collective-permute-done | bytes 1056800 | tf_op jit(solution)/shard_map/ppermute | solution.py:430
  45.4 6.5 %shard_map.158 = (f32[1032,256]{1,0:T(8,128)}, f32[4,256,256]{2,1,0:T(8,128)}, f32[2048,256]{1,0:T(8,128)}) custom-call(s32[1,4,16]{2,1,0:T(4,128)} %lefts.15, s32[1,4,16]{2,1,0:T(4,128)} %rights.15, s32[1,4,16]{2,1,0:T(4,128)} %kinds.15, s32[1,4]{1,0:T(1,128)} %count.15, ...), custom_call_target="tpu_custom_call", output_to_operand_aliasing={{0}: (6, {}), {1}: (8, {})} | custom-call | flops 4000000000 | bytes 2097152 | tf_op jit(solution)/shard_map/pallas_call | solution.py:361
  51.9 2.0 %collective-permute-start.5 = (f32[1032,256]{1,0:T(8,128)}, f32[1032,256]{1,0:T(8,128)}, u32[]{:S(2)}, u32[]{:S(2)}) collective-permute-start(f32[1032,256]{1,0:T(8,128)} %get-tuple-element.65), channel_id=1, source_target_pairs={{0,1},{1,2},{2,3},{3,4},{4,5},{5,6},{6,7},{7,8},{8,9},{9,10},{10,1... | collective-permute-start | bytes 3170312 | tf_op jit(solution)/shard_map/ppermute | solution.py:430
  54.0 2.8 %collective-permute-done.2.refs_2_ = f32[1032,256]{1,0:T(8,128)} collective-permute-done((f32[1032,256]{1,0:T(8,128)}, f32[1032,256]{1,0:T(8,128)}, u32[]{:S(2)}, u32[]{:S(2)}) %collective-permute-start.2) | collective-permute-done | bytes 1056800 | tf_op jit(solution)/shard_map/ppermute | solution.py:430
  56.8 7.1 %shard_map.159 = (f32[2048,256]{1,0:T(8,128)}, f32[16,128]{1,0:T(8,128)}, f32[1032,256]{1,0:T(8,128)}, f32[4,256,256]{2,1,0:T(8,128)}) custom-call(s32[1,4,16]{2,1,0:T(4,128)} %lefts.15, s32[1,4,16]{2,1,0:T(4,128)} %rights.15, s32[1,4,16]{2,1,0:T(4,128)} %kinds.15, ...), custom_call_target="tpu_custom_call", output_to_operand_aliasing={{0}: (5, {}), {1}: (6, {}), {2}: (7, {}), {3}: (9, {})} | custom-call | flops 4000000000 | bytes 2097152 | tf_op jit(solution)/shard_map/pallas_call | solution.py:361
  63.9 4.1 %collective-permute-start.4 = (f32[1032,256]{1,0:T(8,128)}, f32[1032,256]{1,0:T(8,128)}, u32[]{:S(2)}, u32[]{:S(2)}) collective-permute-start(f32[1032,256]{1,0:T(8,128)} %get-tuple-element.64), channel_id=1, source_target_pairs={{0,1},{1,2},{2,3},{3,4},{4,5},{5,6},{6,7},{7,8},{8,9},{9,10},{10,1... | collective-permute-start | bytes 3170312 | tf_op jit(solution)/shard_map/ppermute | solution.py:430
  68.0 0.1 collective-permute-done.5.refs_1_
  68.1 5.7 %shard_map.160 = (f32[1032,256]{1,0:T(8,128)}, f32[4,256,256]{2,1,0:T(8,128)}, f32[2048,256]{1,0:T(8,128)}) custom-call(s32[1,4,16]{2,1,0:T(4,128)} %lefts.15, s32[1,4,16]{2,1,0:T(4,128)} %rights.15, s32[1,4,16]{2,1,0:T(4,128)} %kinds.15, s32[1,4]{1,0:T(1,128)} %count.15, ...), custom_call_target="tpu_custom_call", output_to_operand_aliasing={{0}: (6, {}), {1}: (8, {})} | custom-call | flops 4000000000 | bytes 2097152 | tf_op jit(solution)/shard_map/pallas_call | solution.py:361
  73.8 0.1 collective-permute-start.7
  73.9 6.7 %collective-permute-done.4.refs_2_ = f32[1032,256]{1,0:T(8,128)} collective-permute-done((f32[1032,256]{1,0:T(8,128)}, f32[1032,256]{1,0:T(8,128)}, u32[]{:S(2)}, u32[]{:S(2)}) %collective-permute-start.4) | collective-permute-done | bytes 1056800 | tf_op jit(solution)/shard_map/ppermute | solution.py:430
  80.6 6.6 %shard_map.161 = (f32[2048,256]{1,0:T(8,128)}, f32[16,128]{1,0:T(8,128)}, f32[1032,256]{1,0:T(8,128)}, f32[4,256,256]{2,1,0:T(8,128)}) custom-call(s32[1,4,16]{2,1,0:T(4,128)} %lefts.15, s32[1,4,16]{2,1,0:T(4,128)} %rights.15, s32[1,4,16]{2,1,0:T(4,128)} %kinds.15, ...), custom_call_target="tpu_custom_call", output_to_operand_aliasing={{0}: (5, {}), {1}: (6, {}), {2}: (7, {}), {3}: (9, {})} | custom-call | flops 4000000000 | bytes 2097152 | tf_op jit(solution)/shard_map/pallas_call | solution.py:361
  87.3 0.0 copy-start.1
  87.3 1.2 dynamic-slice_bitcast_fusion
  88.5 0.1 collective-permute-start.6
  88.6 1.9 %collective-permute-done.6 = f32[512,256]{1,0:T(8,128)S(1)} collective-permute-done((f32[512,256]{1,0:T(8,128)S(1)}, f32[512,256]{1,0:T(8,128)S(1)}, u32[]{:S(2)}, u32[]{:S(2)}) %collective-permute-start.6) | collective-permute-done | bytes 524320 | tf_op jit(solution)/shard_map/ppermute | solution.py:465
  90.5 0.0 copy-done.1
  90.5 0.1 bitcast_add_fusion
  90.5 1.3 collective-permute-start.14
  91.9 3.9 %collective-permute-done.7.refs_0_ = f32[1032,256]{1,0:T(8,128)} collective-permute-done((f32[1032,256]{1,0:T(8,128)}, f32[1032,256]{1,0:T(8,128)}, u32[]{:S(2)}, u32[]{:S(2)}) %collective-permute-start.7) | collective-permute-done | bytes 1056800 | tf_op jit(solution)/shard_map/ppermute | solution.py:430
  95.8 8.6 %collective-permute-start.10 = (f32[128,256]{1,0:T(8,128)S(1)}, f32[128,256]{1,0:T(8,128)S(1)}, u32[]{:S(2)}, u32[]{:S(2)}) collective-permute-start(f32[128,256]{1,0:T(8,128)S(1)} %get-tuple-element.91), channel_id=1, source_target_pairs={{0,6},{1,7},{2,4},{3,5},{4,2},{5,3},{6,0},{7,1},{8,14},{9,15},{10,... | collective-permute-start | bytes 393224 | tf_op jit(solution)/shard_map/ppermute | solution.py:465
  104.4 0.0 collective-permute-start.8
  104.4 0.4 collective-permute-start.9
  104.8 2.1 %collective-permute-done.10 = f32[128,256]{1,0:T(8,128)S(1)} collective-permute-done((f32[128,256]{1,0:T(8,128)S(1)}, f32[128,256]{1,0:T(8,128)S(1)}, u32[]{:S(2)}, u32[]{:S(2)}) %collective-permute-start.10) | collective-permute-done | bytes 131104 | tf_op jit(solution)/shard_map/ppermute | solution.py:465
  106.9 1.8 %collective-permute-done.8 = f32[128,256]{1,0:T(8,128)S(1)} collective-permute-done((f32[128,256]{1,0:T(8,128)S(1)}, f32[128,256]{1,0:T(8,128)S(1)}, u32[]{:S(2)}, u32[]{:S(2)}) %collective-permute-start.8) | collective-permute-done | bytes 131104 | tf_op jit(solution)/shard_map/ppermute | solution.py:465
  108.7 7.4 %collective-permute-done.9 = f32[128,256]{1,0:T(8,128)S(1)} collective-permute-done((f32[128,256]{1,0:T(8,128)S(1)}, f32[128,256]{1,0:T(8,128)S(1)}, u32[]{:S(2)}, u32[]{:S(2)}) %collective-permute-start.9) | collective-permute-done | bytes 131104 | tf_op jit(solution)/shard_map/ppermute | solution.py:465
  116.1 7.7 %collective-permute-start.11 = (f32[128,256]{1,0:T(8,128)S(1)}, f32[128,256]{1,0:T(8,128)S(1)}, u32[]{:S(2)}, u32[]{:S(2)}) collective-permute-start(f32[128,256]{1,0:T(8,128)S(1)} %fusion.1), channel_id=1, source_target_pairs={{0,8},{1,9},{2,10},{3,11},{4,12},{5,13},{6,14},{7,15},{8,0},{9,1},... | collective-permute-start | bytes 393224 | tf_op jit(solution)/shard_map/ppermute | solution.py:472
  123.8 0.0 collective-permute-start.12
  123.8 1.3 collective-permute-start.13
  125.1 3.9 %collective-permute-start.18 = (f32[1032,256]{1,0:T(8,128)}, f32[1032,256]{1,0:T(8,128)S(1)}, u32[]{:S(2)}, u32[]{:S(2)}) collective-permute-start(f32[1032,256]{1,0:T(8,128)} %get-tuple-element.81), channel_id=1, source_target_pairs={{1,30},{3,0},{5,2},{7,4},{9,6},{11,8},{13,10},{15,12},{17,14},{19,... | collective-permute-start | bytes 3170312 | tf_op jit(solution)/shard_map/ppermute | solution.py:430
  129.0 0.0 collective-permute-done.11
  129.0 0.4 collective-permute-done.12
  129.4 19.0 %collective-permute-done.13 = f32[128,256]{1,0:T(8,128)S(1)} collective-permute-done((f32[128,256]{1,0:T(8,128)S(1)}, f32[128,256]{1,0:T(8,128)S(1)}, u32[]{:S(2)}, u32[]{:S(2)}) %collective-permute-start.13) | collective-permute-done | bytes 131104 | tf_op jit(solution)/shard_map/ppermute | solution.py:472
  148.4 0.0 collective-permute-done.14.refs_1_
  148.4 0.1 collective-permute-start.15
  148.5 0.1 collective-permute-start.16
  148.6 2.6 %collective-permute-start.17 = (f32[128,256]{1,0:T(8,128)S(1)}, f32[128,256]{1,0:T(8,128)S(1)}, u32[]{:S(2)}, u32[]{:S(2)}) collective-permute-start(f32[128,256]{1,0:T(8,128)S(1)} %add_add_fusion), channel_id=1, source_target_pairs={{0,6},{1,7},{2,4},{3,5},{4,2},{5,3},{6,0},{7,1},{8,14},{9,15},{10,... | collective-permute-start | bytes 393224 | tf_op jit(solution)/shard_map/ppermute | solution.py:479
  151.2 1.1 collective-permute-done.15
  152.3 3.3 %collective-permute-done.16 = f32[128,256]{1,0:T(8,128)S(1)} collective-permute-done((f32[128,256]{1,0:T(8,128)S(1)}, f32[128,256]{1,0:T(8,128)S(1)}, u32[]{:S(2)}, u32[]{:S(2)}) %collective-permute-start.16) | collective-permute-done | bytes 131104 | tf_op jit(solution)/shard_map/ppermute | solution.py:479
  155.6 0.0 collective-permute-done.17
  155.7 0.0 collective-permute-done.18.refs_2_
  155.7 1.7 %collective-permute-start.19 = (f32[512,256]{1,0:T(8,128)S(1)}, f32[512,256]{1,0:T(8,128)S(1)}, u32[]{:S(2)}, u32[]{:S(2)}) collective-permute-start(f32[512,256]{1,0:T(8,128)S(1)} %bitcast.40), channel_id=1, source_target_pairs={{0,1},{1,0},{2,3},{3,2},{4,5},{5,4},{6,7},{7,6},{8,9},{9,8},{10,11... | collective-permute-start | bytes 1572872 | tf_op jit(solution)/shard_map/ppermute | solution.py:479
  157.4 2.6 %shard_map.162 = (f32[2048,256]{1,0:T(8,128)}, f32[16,128]{1,0:T(8,128)}) custom-call(s32[1]{0:T(128)} %bitcast.3.turn, f32[1032,256]{1,0:T(8,128)} %collective-permute-done.7.refs_0_, f32[1032,256]{1,0:T(8,128)S(1)} %collective-permute-done.14.refs_1_, f32[1032,256]{1,0:T(8,128)S(1)} %collective-permute-done.18.refs_2_), custom_call_target="tpu_custom_call" | custom-call | tf_op jit(solution)/shard_map/pallas_call | solution.py:418
  160.0 0.1 broadcast_in_dim.32
  160.1 0.0 collective-permute-done.19
  160.2 0.0 copy-start.2
  160.2 0.0 copy-start
  160.2 0.2 multiply_reduce_fusion
  160.4 0.4 copy-done.2
  160.9 0.6 sqrt_add_fusion
  161.5 0.0 copy-done
  161.5 1.2 divide_subtract_fusion
  (12 shorter events, 0.3 us)
Async XLA Ops:
  6.6 16.2 %collective-permute-start.1 = (f32[1032,256]{1,0:T(8,128)}, f32[1032,256]{1,0:T(8,128)}, u32[]{:S(2)}, u32[]{:S(2)}) collective-permute-start(f32[1032,256]{1,0:T(8,128)} %get-tuple-element.51), channel_id=1, source_target_pairs={{0,1},{1,2},{2,3},{3,4},{4,5},{5,6},{6,7},{7,8},{8,9},{9,10},{10,1... | collective-permute-start | bytes 3170312 | tf_op jit(solution)/shard_map/ppermute | solution.py:430
  15.7 18.5 %collective-permute-start = (f32[1032,256]{1,0:T(8,128)}, f32[1032,256]{1,0:T(8,128)}, u32[]{:S(2)}, u32[]{:S(2)}) collective-permute-start(f32[1032,256]{1,0:T(8,128)} %get-tuple-element.50), channel_id=1, source_target_pairs={{0,1},{1,2},{2,3},{3,4},{4,5},{5,6},{6,7},{7,8},{8,9},{9,10},{10,1... | collective-permute-start | bytes 3170312 | tf_op jit(solution)/shard_map/ppermute | solution.py:430
  28.7 16.8 %collective-permute-start.3 = (f32[1032,256]{1,0:T(8,128)}, f32[1032,256]{1,0:T(8,128)}, u32[]{:S(2)}, u32[]{:S(2)}) collective-permute-start(f32[1032,256]{1,0:T(8,128)} %get-tuple-element.58), channel_id=1, source_target_pairs={{0,1},{1,2},{2,3},{3,4},{4,5},{5,6},{6,7},{7,8},{8,9},{9,10},{10,1... | collective-permute-start | bytes 3170312 | tf_op jit(solution)/shard_map/ppermute | solution.py:430
  40.4 16.3 %collective-permute-start.2 = (f32[1032,256]{1,0:T(8,128)}, f32[1032,256]{1,0:T(8,128)}, u32[]{:S(2)}, u32[]{:S(2)}) collective-permute-start(f32[1032,256]{1,0:T(8,128)} %get-tuple-element.57), channel_id=1, source_target_pairs={{0,1},{1,2},{2,3},{3,4},{4,5},{5,6},{6,7},{7,8},{8,9},{9,10},{10,1... | collective-permute-start | bytes 3170312 | tf_op jit(solution)/shard_map/ppermute | solution.py:430
  51.9 16.2 %collective-permute-start.5 = (f32[1032,256]{1,0:T(8,128)}, f32[1032,256]{1,0:T(8,128)}, u32[]{:S(2)}, u32[]{:S(2)}) collective-permute-start(f32[1032,256]{1,0:T(8,128)} %get-tuple-element.65), channel_id=1, source_target_pairs={{0,1},{1,2},{2,3},{3,4},{4,5},{5,6},{6,7},{7,8},{8,9},{9,10},{10,1... | collective-permute-start | bytes 3170312 | tf_op jit(solution)/shard_map/ppermute | solution.py:430
  63.9 16.7 %collective-permute-start.4 = (f32[1032,256]{1,0:T(8,128)}, f32[1032,256]{1,0:T(8,128)}, u32[]{:S(2)}, u32[]{:S(2)}) collective-permute-start(f32[1032,256]{1,0:T(8,128)} %get-tuple-element.64), channel_id=1, source_target_pairs={{0,1},{1,2},{2,3},{3,4},{4,5},{5,6},{6,7},{7,8},{8,9},{9,10},{10,1... | collective-permute-start | bytes 3170312 | tf_op jit(solution)/shard_map/ppermute | solution.py:430
  73.8 21.9 %collective-permute-start.7 = (f32[1032,256]{1,0:T(8,128)}, f32[1032,256]{1,0:T(8,128)}, u32[]{:S(2)}, u32[]{:S(2)}) collective-permute-start(f32[1032,256]{1,0:T(8,128)} %get-tuple-element.74), channel_id=1, source_target_pairs={{0,29},{1,30},{2,31},{3,0},{4,1},{5,2},{6,3},{7,4},{8,5},{9,6},{10... | collective-permute-start | bytes 3170312 | tf_op jit(solution)/shard_map/ppermute | solution.py:430
  87.3 3.2 %copy-start.1 = (f32[4,256,256]{2,1,0:T(8,128)S(1)}, f32[4,256,256]{2,1,0:T(8,128)}, u32[]{:S(2)}) copy-start(f32[4,256,256]{2,1,0:T(8,128)} %get-tuple-element.71) | copy-start | bytes 3145732
  88.5 2.0 %collective-permute-start.6 = (f32[512,256]{1,0:T(8,128)S(1)}, f32[512,256]{1,0:T(8,128)S(1)}, u32[]{:S(2)}, u32[]{:S(2)}) collective-permute-start(f32[512,256]{1,0:T(8,128)S(1)} %dynamic-slice_bitcast_fusion), channel_id=1, source_target_pairs={{0,1},{1,0},{2,3},{3,2},{4,5},{5,4},{6,7},{7,6},{8,9},{9,8},{10,11... | collective-permute-start | bytes 1572872 | tf_op jit(solution)/shard_map/ppermute | solution.py:465
  90.5 57.9 %collective-permute-start.14 = (f32[1032,256]{1,0:T(8,128)}, f32[1032,256]{1,0:T(8,128)S(1)}, u32[]{:S(2)}, u32[]{:S(2)}) collective-permute-start(f32[1032,256]{1,0:T(8,128)} %get-tuple-element.81), channel_id=1, source_target_pairs={{0,29},{2,31},{4,1},{6,3},{8,5},{10,7},{12,9},{14,11},{16,13},{18,... | collective-permute-start | bytes 3170312 | tf_op jit(solution)/shard_map/ppermute | solution.py:430
  95.8 11.1 %collective-permute-start.10 = (f32[128,256]{1,0:T(8,128)S(1)}, f32[128,256]{1,0:T(8,128)S(1)}, u32[]{:S(2)}, u32[]{:S(2)}) collective-permute-start(f32[128,256]{1,0:T(8,128)S(1)} %get-tuple-element.91), channel_id=1, source_target_pairs={{0,6},{1,7},{2,4},{3,5},{4,2},{5,3},{6,0},{7,1},{8,14},{9,15},{10,... | collective-permute-start | bytes 393224 | tf_op jit(solution)/shard_map/ppermute | solution.py:465
  104.4 4.3 %collective-permute-start.8 = (f32[128,256]{1,0:T(8,128)S(1)}, f32[128,256]{1,0:T(8,128)S(1)}, u32[]{:S(2)}, u32[]{:S(2)}) collective-permute-start(f32[128,256]{1,0:T(8,128)S(1)} %get-tuple-element.90), channel_id=1, source_target_pairs={{0,2},{1,3},{2,0},{3,1},{4,6},{5,7},{6,4},{7,5},{8,10},{9,11},{10,... | collective-permute-start | bytes 393224 | tf_op jit(solution)/shard_map/ppermute | solution.py:465
  104.4 11.7 %collective-permute-start.9 = (f32[128,256]{1,0:T(8,128)S(1)}, f32[128,256]{1,0:T(8,128)S(1)}, u32[]{:S(2)}, u32[]{:S(2)}) collective-permute-start(f32[128,256]{1,0:T(8,128)S(1)} %get-tuple-element.92), channel_id=1, source_target_pairs={{0,4},{1,5},{2,6},{3,7},{4,0},{5,1},{6,2},{7,3},{8,12},{9,13},{10,... | collective-permute-start | bytes 393224 | tf_op jit(solution)/shard_map/ppermute | solution.py:465
  116.1 12.8 %collective-permute-start.11 = (f32[128,256]{1,0:T(8,128)S(1)}, f32[128,256]{1,0:T(8,128)S(1)}, u32[]{:S(2)}, u32[]{:S(2)}) collective-permute-start(f32[128,256]{1,0:T(8,128)S(1)} %fusion.1), channel_id=1, source_target_pairs={{0,8},{1,9},{2,10},{3,11},{4,12},{5,13},{6,14},{7,15},{8,0},{9,1},... | collective-permute-start | bytes 393224 | tf_op jit(solution)/shard_map/ppermute | solution.py:472
  123.8 5.5 %collective-permute-start.12 = (f32[128,256]{1,0:T(8,128)S(1)}, f32[128,256]{1,0:T(8,128)S(1)}, u32[]{:S(2)}, u32[]{:S(2)}) collective-permute-start(f32[128,256]{1,0:T(8,128)S(1)} %fusion.1), channel_id=1, source_target_pairs={{0,16},{1,17},{2,18},{3,19},{4,20},{5,21},{6,22},{7,23},{8,24},{9,... | collective-permute-start | bytes 393224 | tf_op jit(solution)/shard_map/ppermute | solution.py:472
  123.8 24.5 %collective-permute-start.13 = (f32[128,256]{1,0:T(8,128)S(1)}, f32[128,256]{1,0:T(8,128)S(1)}, u32[]{:S(2)}, u32[]{:S(2)}) collective-permute-start(f32[128,256]{1,0:T(8,128)S(1)} %fusion.1), channel_id=1, source_target_pairs={{0,24},{1,25},{2,26},{3,27},{4,28},{5,29},{6,30},{7,31},{8,16},{9,... | collective-permute-start | bytes 393224 | tf_op jit(solution)/shard_map/ppermute | solution.py:472
  125.1 30.6 %collective-permute-start.18 = (f32[1032,256]{1,0:T(8,128)}, f32[1032,256]{1,0:T(8,128)S(1)}, u32[]{:S(2)}, u32[]{:S(2)}) collective-permute-start(f32[1032,256]{1,0:T(8,128)} %get-tuple-element.81), channel_id=1, source_target_pairs={{1,30},{3,0},{5,2},{7,4},{9,6},{11,8},{13,10},{15,12},{17,14},{19,... | collective-permute-start | bytes 3170312 | tf_op jit(solution)/shard_map/ppermute | solution.py:430
  148.4 3.9 %collective-permute-start.15 = (f32[128,256]{1,0:T(8,128)S(1)}, f32[128,256]{1,0:T(8,128)S(1)}, u32[]{:S(2)}, u32[]{:S(2)}) collective-permute-start(f32[128,256]{1,0:T(8,128)S(1)} %add_add_fusion), channel_id=1, source_target_pairs={{0,2},{1,3},{2,0},{3,1},{4,6},{5,7},{6,4},{7,5},{8,10},{9,11},{10,... | collective-permute-start | bytes 393224 | tf_op jit(solution)/shard_map/ppermute | solution.py:479
  148.5 7.1 %collective-permute-start.16 = (f32[128,256]{1,0:T(8,128)S(1)}, f32[128,256]{1,0:T(8,128)S(1)}, u32[]{:S(2)}, u32[]{:S(2)}) collective-permute-start(f32[128,256]{1,0:T(8,128)S(1)} %add_add_fusion), channel_id=1, source_target_pairs={{0,4},{1,5},{2,6},{3,7},{4,0},{5,1},{6,2},{7,3},{8,12},{9,13},{10,... | collective-permute-start | bytes 393224 | tf_op jit(solution)/shard_map/ppermute | solution.py:479
  148.6 7.1 %collective-permute-start.17 = (f32[128,256]{1,0:T(8,128)S(1)}, f32[128,256]{1,0:T(8,128)S(1)}, u32[]{:S(2)}, u32[]{:S(2)}) collective-permute-start(f32[128,256]{1,0:T(8,128)S(1)} %add_add_fusion), channel_id=1, source_target_pairs={{0,6},{1,7},{2,4},{3,5},{4,2},{5,3},{6,0},{7,1},{8,14},{9,15},{10,... | collective-permute-start | bytes 393224 | tf_op jit(solution)/shard_map/ppermute | solution.py:479
  155.7 4.5 %collective-permute-start.19 = (f32[512,256]{1,0:T(8,128)S(1)}, f32[512,256]{1,0:T(8,128)S(1)}, u32[]{:S(2)}, u32[]{:S(2)}) collective-permute-start(f32[512,256]{1,0:T(8,128)S(1)} %bitcast.40), channel_id=1, source_target_pairs={{0,1},{1,0},{2,3},{3,2},{4,5},{5,4},{6,7},{7,6},{8,9},{9,8},{10,11... | collective-permute-start | bytes 1572872 | tf_op jit(solution)/shard_map/ppermute | solution.py:479
  160.2 0.7 copy-start.2
  160.2 1.3 copy-start
